TPU v7x, 32 devices: a whole 2x2x4 slice. The times are simulated.
32 devices in a mesh: tok: 8 (over z, y), grp: 4 (over x, core).
Axes of the slice: x: 2, y: 2, z: 4, core: 2. Of those that a mesh axis runs over, the one named last changes fastest.
Arguments:
- tokens: bfloat16 [12288, 1024], P(('tok', 'grp')), may hold values from -6 to 6
- norm_gain: float32 [1024], replicated, may hold values from 0.25 to 1.75
- input_weight: bfloat16 [1024, 3072], P('tok', 'grp')
- output_weight: bfloat16 [1024, 1024], P('tok', 'grp'), may hold values from -2 to 2
- segment_ids: int32 [12288], replicated, may hold values from 0 to 23, never falling along the last dimension, each value on 1 to 1024 neighbouring positions
- page_owner: int32 [3072, 1], P(('tok', 'grp')), may hold values from 0 to 7; in each aligned block of 96 rows (0 to 95, 96 to 191, ...) at most 24 rows name the same one
Outputs:
- attended: bfloat16 [12288, 1024], P(('tok', 'grp'))
- cache_pages: bfloat16 [6144, 8192], P(('tok', 'grp'))
Inputs may be any that keep to these rules, and one draw needn't show every extreme that they name: `segment_ids`: segment ids never fall along the pack; every id occurs on 1 to 1024 consecutive tokens, and some document has exactly 1024 tokens. `page_owner`: within the 96 pages of one device no owner is named more than 24 times, and in some device one owner is named exactly 24 times.
All inputs are finite; a program needn't handle non-finite values.
Results may differ from a plain program's by a relative error of at most 0.0089.
Values may be sent and summed in bfloat16 or wider, within the bound.
No kernel may reach another device: no remote copies, remote signals or barrier semaphores. Data moves between devices by JAX's collectives and lax.ppermute only.
A program may use at most 128 MiB of HBM per device.

v0:
```python
import jax
import jax.numpy as jnp
from jax import lax
from jax.sharding import PartitionSpec as P

H = 16
SPAN = 1024
PAGE = 4


NEG_FILL = -1e30
ROPE_BASE = 160000.0
EPSILON = 1e-05


def shifted(value, axis, steps):
    count = lax.axis_size(axis)
    initial, last = (max(0, -steps), min(count, count - steps))
    return lax.ppermute(value, axis, [(source, source + steps) for source in range(initial, last)])


def layer_norm(tokens, norm_gain):
    values = tokens.astype(jnp.float32)
    center = jnp.mean(values, axis=-1, keepdims=True)
    spread = jnp.mean(jnp.square(values - center), axis=-1, keepdims=True)
    return ((values - center) * lax.rsqrt(spread + EPSILON) * norm_gain).astype(jnp.bfloat16)


def rotate(block_part, positions, head_count):
    row_count = block_part.shape[0]
    head_dim = block_part.shape[1] // head_count
    half_dim = head_dim // 2
    shaped = block_part.reshape(row_count, head_count, head_dim)
    inverse = 1.0 / ROPE_BASE ** (jnp.arange(half_dim, dtype=jnp.float32) * 2.0 / head_dim)
    angles = positions.astype(jnp.float32)[:, None] * inverse[None, :]
    cosine = jnp.concatenate([jnp.cos(angles), jnp.cos(angles)], axis=1)[:, None, :]
    sine_table = jnp.concatenate([jnp.sin(angles), jnp.sin(angles)], axis=1)[:, None, :]
    turned = jnp.concatenate([-shaped[..., half_dim:], shaped[..., :half_dim]], axis=-1)
    return (
        (shaped * cosine + turned * sine_table)
        .reshape(row_count, head_count * head_dim)
        .astype(jnp.bfloat16)
    )


def positions_of(segment_ids, own_ids, first_row):
    starts = jnp.searchsorted(segment_ids, own_ids, side="left")
    return first_row + jnp.arange(own_ids.shape[0], dtype=jnp.int32) - starts


def pair_scores(query_pair, key_pair, score_scale):
    return (
        jnp.einsum("tnd,snd->nts", query_pair, key_pair, preferred_element_type=jnp.float32)
        * score_scale
    )


def attend_pairs(queries, key_window, value_window, allowed, head_count):
    row_count = queries.shape[0]
    window_len = key_window.shape[0]
    head_dim = queries.shape[1] // head_count
    pair_count = head_count // 2
    score_scale = head_dim ** (-0.5)
    query_stack = jnp.transpose(queries.reshape(row_count, pair_count, 2, head_dim), (1, 0, 2, 3))
    key_stack = jnp.transpose(key_window.reshape(window_len, pair_count, 2, head_dim), (1, 0, 2, 3))
    value_stack = jnp.transpose(
        value_window.reshape(window_len, pair_count, 2, head_dim), (1, 0, 2, 3)
    )

    def one_pair(operands):
        query_pair, key_pair, value_pair = operands
        scores = jnp.where(allowed[None], pair_scores(query_pair, key_pair, score_scale), NEG_FILL)
        row_peak = jnp.max(scores, axis=-1, keepdims=True)
        exponent = jnp.exp(scores - row_peak)
        row_total = jnp.sum(exponent, axis=-1)
        weights = exponent.astype(jnp.bfloat16)
        mixed_rows = jnp.einsum(
            "nts,snd->tnd", weights, value_pair, preferred_element_type=jnp.float32
        )
        return mixed_rows / jnp.transpose(row_total)[:, :, None]

    mixed_stack = lax.map(one_pair, (query_stack, key_stack, value_stack))
    return (
        jnp.transpose(mixed_stack, (1, 0, 2, 3))
        .reshape(row_count, head_count * head_dim)
        .astype(jnp.bfloat16)
    )


def per_device(tokens, norm_gain, input_weight, output_weight, segment_ids, page_owner):
    row_count = tokens.shape[0]
    model_width = tokens.shape[1]
    device = lax.axis_index(("tok", "grp"))
    first_row = device * row_count
    normed = layer_norm(tokens, norm_gain)
    input_cols, output_cols = (
        lax.all_gather(input_weight, "grp", axis=1, tiled=True),
        lax.all_gather(output_weight, "grp", axis=1, tiled=True),
    )
    section = normed
    joined = jnp.dot(
        section,
        lax.all_gather(input_cols, "tok", axis=0, tiled=True),
        preferred_element_type=jnp.float32,
    )
    own_ids = lax.dynamic_slice_in_dim(segment_ids, first_row, row_count, 0)
    positions = positions_of(segment_ids, own_ids, first_row)
    queries = rotate(joined[:, :model_width], positions, H)
    key_rows = rotate(joined[:, model_width : 2 * model_width], positions, H)
    value_rows = joined[:, 2 * model_width :].astype(jnp.bfloat16)
    paired = jnp.stack([key_rows, value_rows])
    reach_blocks = (SPAN + row_count - 2) // row_count
    window_len = (2 * reach_blocks + 1) * row_count
    earlier = [shifted(paired, ("tok", "grp"), distance) for distance in range(reach_blocks, 0, -1)]
    later_blocks = [
        shifted(paired, ("tok", "grp"), -distance) for distance in range(1, reach_blocks + 1)
    ]
    window = jnp.concatenate(earlier + [paired] + later_blocks, axis=1)
    filler = jnp.full((reach_blocks * row_count,), -1, jnp.int32)
    padded_ids = jnp.concatenate([filler, segment_ids, filler])
    window_ids = lax.dynamic_slice_in_dim(padded_ids, first_row, window_len, 0)
    allowed = own_ids[:, None] == window_ids[None, :]
    mixed_rows = attend_pairs(queries, window[0], window[1], allowed, H)
    section = mixed_rows
    attended = jnp.dot(
        section,
        lax.all_gather(output_cols, "tok", axis=0, tiled=True),
        preferred_element_type=jnp.float32,
    ).astype(jnp.bfloat16)
    page_rows = jnp.concatenate([key_rows, value_rows], axis=1).reshape(
        row_count // PAGE, 2 * PAGE * model_width
    )
    owners = page_owner[:, 0]
    page_count = owners.shape[0]
    earlier_mask = jnp.arange(page_count)[:, None] > jnp.arange(page_count)[None, :]
    page_ranks = jnp.sum(
        ((owners[:, None] == owners[None, :]) & earlier_mask).astype(jnp.int32), axis=1
    )
    peer_count = lax.axis_size("tok")
    capacity = max(2, (2 * page_count + peer_count - 1) // peer_count)
    send_slots = jnp.zeros((peer_count * capacity, page_rows.shape[1]), jnp.bfloat16)
    send_slots = send_slots.at[owners * capacity + page_ranks].set(page_rows)
    cache_pages = lax.all_to_all(send_slots, "tok", split_axis=0, concat_axis=0, tiled=True)
    return (attended, cache_pages)


def solution(mesh):
    placed = (
        P(("tok", "grp"), None),
        P(),
        P("tok", "grp"),
        P("tok", "grp"),
        P(),
        P(("tok", "grp"), None),
    )
    return jax.shard_map(
        per_device,
        mesh=mesh,
        in_specs=placed,
        out_specs=(P(("tok", "grp"), None), P(("tok", "grp"), None)),
        check_vma=False,
    )
```

profile of v0, /device:TPU:3, one launch (start us, length us, event | category | flops | bytes accessed | tf_op | source)
XLA Modules:
  0.0 465.4 jit_solution(16861483362091834658)
XLA Ops:
  7.2 9.4 %all_gather.12 = bf16[128,3072]{1,0:T(8,128)(2,1)} all-gather(bf16[128,768]{1,0:T(8,128)(2,1)} %param.12), channel_id=1, replica_groups=mesh['tok'=8,'grp'=4] {'grp'}, dimensions={1}, use_global_device_ids=true | all-gather | bytes 983040 | tf_op jit(solution)/shard_map/all_gather | solution.py:97
  17.5 50.0 %while.36 = (s32[]{:T(128)}, u32[384]{0:T(512)S(1)}, u32[384]{0:T(512)S(1)}, s32[12288]{0:T(1024)}, s32[384]{0:T(512)S(1)}, /*index=5*/s32[]{:T(128)}, s32[]{:T(128)}, s32[]{}) while((s32[]{:T(128)}, u32[384]{0:T(512)S(1)}, u32[384]{0:T(512)S(1)}, s32[12288]{0:T(1024)}, s32[384]{0:T(512)S(1)}, /*index=5*/s32[]{:T(128)}, s32[]{:T(128)}, ...), condition=%wide.region_3.4_spmd.clone, body=%wide.region_2.3_spmd.clone.sunk | while | flops 7940 | bytes 31085 | solution.py:47
  24.6 3.5 gather_fusion
  28.2 3.5 gather_fusion
  31.8 3.5 gather_fusion
  35.4 3.5 gather_fusion
  38.9 3.5 gather_fusion
  46.1 3.5 gather_fusion
  49.6 3.5 gather_fusion
  53.2 3.5 gather_fusion
  60.4 3.5 gather_fusion
  70.1 46.4 %all-gather.3.cloned.1.call-done = bf16[1024,3072]{1,0:T(8,128)(2,1)} async-done(((bf16[128,3072]{1,0:T(8,128)(2,1)}), bf16[1024,3072]{1,0:T(8,128)(2,1)}) %all-gather.3.cloned.1.call-update) | async-done | bytes 6291472 | tf_op jit(solution)/shard_map/all_gather | solution.py:103
  116.5 4.9 %fusion.38 = f32[384,3072]{1,0:T(8,128)S(1)} fusion(bf16[1024,3072]{1,0:T(8,128)(2,1)} %all-gather.3.cloned.1.call-done, bf16[384,1024]{1,0:T(8,128)(2,1)S(1)} %copy-done.6, f32[1024]{0:T(1024)S(1)} %copy-done.8, f32[384]{0:T(512)S(1)} %add_rsqrt_fusion, f32[384]{0:T(512)S(1)} %broadcast_multiply_fusion), kind=kOutput, calls=%fused_computation.47 | convolution fusion | flops 2417885184 | bytes 11803648 | tf_op jit(solution)/shard_map/dot_general | solution.py:101
  141.6 4.2 add_convert_fusion
  157.7 4.7 %collective-permute-start.4 = (bf16[2,384,1024]{2,1,0:T(8,128)(2,1)}, bf16[2,384,1024]{2,1,0:T(8,128)(2,1)}, u32[]{:S(2)}, u32[]{:S(2)}) collective-permute-start(bf16[2,384,1024]{2,1,0:T(8,128)(2,1)} %pad_maximum_fusion), channel_id=1, source_target_pairs={{2,0},{3,1},{4,2},{5,3},{6,4},{7,5},{8,6},{9,7},{10,8},{11,9},{12,... | collective-permute-start | bytes 4718600 | tf_op jit(solution)/shard_map/ppermute | solution.py:19
  162.4 110.6 %all_gather.14 = bf16[128,1024]{1,0:T(8,128)(2,1)} all-gather(bf16[128,256]{1,0:T(8,128)(2,1)S(1)} %copy-done.7), channel_id=1, replica_groups=mesh['tok'=8,'grp'=4] {'grp'}, dimensions={1}, use_global_device_ids=true | all-gather | bytes 327680 | tf_op jit(solution)/shard_map/all_gather | solution.py:98
  283.6 5.7 %scatter_custom_fusion = bf16[192,8192]{1,0:T(8,128)(2,1)} fusion(s32[96]{0:T(128)S(1)} %fusion.46, bf16[96,8192]{1,0:T(8,128)(2,1)} %reshape.75, bf16[]{:T(256)} %constant.92.clone.1), kind=kCustom, calls=%fused_computation.42 | custom fusion | bytes 3146240 | tf_op jit(solution)/shard_map/scatter | solution.py:142
  289.3 8.5 %all-to-all-start = ((bf16[8,24,8192]{2,1,0:T(8,128)(2,1)}), bf16[8,24,8192]{2,1,0:T(8,128)(2,1)S(1)}, u32[]{:S(2)}, u32[]{:S(2)}) async-start(bf16[8,24,8192]{2,1,0:T(8,128)(2,1)} %bitcast.71), calls=%async_computation | async-start | bytes 6291456 | tf_op jit(solution)/shard_map/all_to_all | solution.py:143
  312.9 29.2 %collective-permute-done.5 = bf16[2,384,1024]{2,1,0:T(8,128)(2,1)} collective-permute-done((bf16[2,384,1024]{2,1,0:T(8,128)(2,1)}, bf16[2,384,1024]{2,1,0:T(8,128)(2,1)}, u32[]{:S(2)}, u32[]{:S(2)}) %collective-permute-start.5) | collective-permute-done | bytes 1572896 | tf_op jit(solution)/shard_map/ppermute | solution.py:19
  344.8 9.5 %fusion.47 = (bf16[1,2688,1024]{2,1,0:T(8,128)(2,1)}, bf16[1,2688,1024]{2,1,0:T(8,128)(2,1)}) fusion(bf16[2,2688,1024]{2,1,0:T(8,128)(2,1)} %constant_dynamic-update-slice_fusion), kind=kLoop, calls=%fused_computation.79 | loop fusion | bytes 22020096 | tf_op jit(solution)/shard_map/slice | solution.py:123
  354.3 7.9 %copy.28 = bf16[1,2688,1024]{1,2,0:T(8,128)(2,1)} copy(bf16[1,2688,1024]{2,1,0:T(8,128)(2,1)} %get-tuple-element.165) | data formatting | bytes 11010048 | tf_op jit(solution)/shard_map/slice | solution.py:123
  362.2 7.9 %copy.23 = bf16[1,2688,1024]{1,2,0:T(8,128)(2,1)} copy(bf16[1,2688,1024]{2,1,0:T(8,128)(2,1)} %get-tuple-element.166) | data formatting | bytes 11010048 | tf_op jit(solution)/shard_map/slice | solution.py:123
  370.1 83.1 %while.35 = (s32[]{:T(128)}, bf16[8,384,2,64]{1,3,2,0:T(8,128)(2,1)}, bf16[8,2688,2,64]{1,3,2,0:T(8,128)(2,1)}, bf16[8,384,2,64]{1,3,2,0:T(8,128)(2,1)}, bf16[8,...) while((s32[]{:T(128)}, bf16[8,384,2,64]{1,3,2,0:T(8,128)(2,1)}, ...), condition=%wide.region_7.8_spmd.clone, body=%wide.region_4.7_spmd.clone.sunk | while | flops 552270336 | bytes 30602324 | solution.py:82
  376.3 4.2 fusion.61
  386.7 4.2 fusion.61
  397.1 4.2 fusion.61
  407.4 4.2 fusion.61
  417.8 4.2 fusion.61
  428.2 4.2 fusion.61
  438.6 4.2 fusion.61
  449.0 4.2 fusion.61
  453.2 3.7 convolution_convert_fusion
  (174 shorter events, 132.7 us)
Async XLA Ops:
  7.2 109.3 %all-gather.3.cloned.1.call-start = ((), (), s32[]{:S(2)}) async-start(), calls=%async_computation.1 | async-start | bytes 7077888 | tf_op jit(solution)/shard_map/all_gather | solution.py:103
  16.6 436.6 %all-gather.5.cloned.1.call-start = ((), (), s32[]{:S(2)}) async-start(), calls=%async_computation.2 | async-start | bytes 2359296 | tf_op jit(solution)/shard_map/all_gather | solution.py:127
  67.5 2.1 copy-start.6
  67.8 48.7 %copy-start.8 = (f32[1024]{0:T(1024)S(1)}, f32[1024]{0:T(1024)}, u32[]{:S(2)}) copy-start(f32[1024]{0:T(1024)} %param.11) | copy-start | bytes 12292
  121.4 3.2 copy-start.1
  124.7 21.1 %copy-start.4 = (bf16[1,384,1024]{2,1,0:T(8,128)(2,1)}, bf16[1,384,1024]{2,1,0:T(8,128)(2,1)S(1)}, u32[]{:S(2)}) copy-start(bf16[1,384,1024]{2,1,0:T(8,128)(2,1)S(1)} %slice_bitcast_fusion) | copy-start | bytes 2359300
  145.8 134.1 %copy-start.2 = (bf16[384,1024]{1,0:T(8,128)(2,1)}, bf16[384,1024]{1,0:T(8,128)(2,1)S(1)}, u32[]{:S(2)}) copy-start(bf16[384,1024]{1,0:T(8,128)(2,1)S(1)} %get-tuple-element.168) | copy-start | bytes 2359300
  145.8 16.6 %copy-start.7 = (bf16[128,256]{1,0:T(8,128)(2,1)S(1)}, bf16[128,256]{1,0:T(8,128)(2,1)}, u32[]{:S(2)}) copy-start(bf16[128,256]{1,0:T(8,128)(2,1)} %param.13) | copy-start | bytes 196612
  145.8 130.1 %copy-start = (s32[12288]{0:T(1024)S(1)}, s32[12288]{0:T(1024)}, u32[]{:S(2)}) copy-start(s32[12288]{0:T(1024)} %get-tuple-element.319) | copy-start | bytes 147460
  145.9 130.2 %copy-start.9 = (s32[96,1]{0,1:T(1,128)S(1)}, s32[96,1]{0,1:T(1,128)}, u32[]{:S(2)}) copy-start(s32[96,1]{0,1:T(1,128)} %param.15) | copy-start | bytes 1156
  147.2 125.8 %collective-permute-start = (bf16[2,384,1024]{2,1,0:T(8,128)(2,1)}, bf16[2,384,1024]{2,1,0:T(8,128)(2,1)}, u32[]{:S(2)}, u32[]{:S(2)}) collective-permute-start(bf16[2,384,1024]{2,1,0:T(8,128)(2,1)} %pad_maximum_fusion), channel_id=1, source_target_pairs={{0,3},{1,4},{2,5},{3,6},{4,7},{5,8},{6,9},{7,10},{8,11},{9,12},{10... | collective-permute-start | bytes 4718600 | tf_op jit(solution)/shard_map/ppermute | solution.py:19
  150.4 150.1 %collective-permute-start.1 = (bf16[2,384,1024]{2,1,0:T(8,128)(2,1)}, bf16[2,384,1024]{2,1,0:T(8,128)(2,1)}, u32[]{:S(2)}, u32[]{:S(2)}) collective-permute-start(bf16[2,384,1024]{2,1,0:T(8,128)(2,1)} %pad_maximum_fusion), channel_id=1, source_target_pairs={{0,2},{1,3},{2,4},{3,5},{4,6},{5,7},{6,8},{7,9},{8,10},{9,11},{10,... | collective-permute-start | bytes 4718600 | tf_op jit(solution)/shard_map/ppermute | solution.py:19
  153.0 150.4 %collective-permute-start.2 = (bf16[2,384,1024]{2,1,0:T(8,128)(2,1)}, bf16[2,384,1024]{2,1,0:T(8,128)(2,1)}, u32[]{:S(2)}, u32[]{:S(2)}) collective-permute-start(bf16[2,384,1024]{2,1,0:T(8,128)(2,1)} %pad_maximum_fusion), channel_id=1, source_target_pairs={{0,1},{1,2},{2,3},{3,4},{4,5},{5,6},{6,7},{7,8},{8,9},{9,10},{10,1... | collective-permute-start | bytes 4718600 | tf_op jit(solution)/shard_map/ppermute | solution.py:19
  155.7 151.8 %collective-permute-start.3 = (bf16[2,384,1024]{2,1,0:T(8,128)(2,1)}, bf16[2,384,1024]{2,1,0:T(8,128)(2,1)}, u32[]{:S(2)}, u32[]{:S(2)}) collective-permute-start(bf16[2,384,1024]{2,1,0:T(8,128)(2,1)} %pad_maximum_fusion), channel_id=1, source_target_pairs={{1,0},{2,1},{3,2},{4,3},{5,4},{6,5},{7,6},{8,7},{9,8},{10,9},{11,1... | collective-permute-start | bytes 4718600 | tf_op jit(solution)/shard_map/ppermute | solution.py:19
  157.7 152.6 %collective-permute-start.4 = (bf16[2,384,1024]{2,1,0:T(8,128)(2,1)}, bf16[2,384,1024]{2,1,0:T(8,128)(2,1)}, u32[]{:S(2)}, u32[]{:S(2)}) collective-permute-start(bf16[2,384,1024]{2,1,0:T(8,128)(2,1)} %pad_maximum_fusion), channel_id=1, source_target_pairs={{2,0},{3,1},{4,2},{5,3},{6,4},{7,5},{8,6},{9,7},{10,8},{11,9},{12,... | collective-permute-start | bytes 4718600 | tf_op jit(solution)/shard_map/ppermute | solution.py:19
  273.0 69.1 %collective-permute-start.5 = (bf16[2,384,1024]{2,1,0:T(8,128)(2,1)}, bf16[2,384,1024]{2,1,0:T(8,128)(2,1)}, u32[]{:S(2)}, u32[]{:S(2)}) collective-permute-start(bf16[2,384,1024]{2,1,0:T(8,128)(2,1)} %pad_maximum_fusion), channel_id=1, source_target_pairs={{3,0},{4,1},{5,2},{6,3},{7,4},{8,5},{9,6},{10,7},{11,8},{12,9},{13... | collective-permute-start | bytes 4718600 | tf_op jit(solution)/shard_map/ppermute | solution.py:19
  289.3 167.6 %all-to-all-start = ((bf16[8,24,8192]{2,1,0:T(8,128)(2,1)}), bf16[8,24,8192]{2,1,0:T(8,128)(2,1)S(1)}, u32[]{:S(2)}, u32[]{:S(2)}) async-start(bf16[8,24,8192]{2,1,0:T(8,128)(2,1)} %bitcast.71), calls=%async_computation | async-start | bytes 6291456 | tf_op jit(solution)/shard_map/all_to_all | solution.py:143
  300.5 5.6 %copy-start.3 = (bf16[384,1024]{1,0:T(8,128)(2,1)S(1)}, bf16[384,1024]{1,0:T(8,128)(2,1)}, u32[]{:S(2)}) copy-start(bf16[384,1024]{1,0:T(8,128)(2,1)} %copy-done.2) | copy-start | bytes 2359300
  300.5 5.6 %copy-start.5 = (bf16[1,384,1024]{2,1,0:T(8,128)(2,1)S(1)}, bf16[1,384,1024]{2,1,0:T(8,128)(2,1)}, u32[]{:S(2)}) copy-start(bf16[1,384,1024]{2,1,0:T(8,128)(2,1)} %copy-done.4) | copy-start | bytes 2359300
Sparse Core Ops, SparseCore 0:
  16.7 99.7 all-gather.2
  273.1 123.5 all-gather.4
where the time goes:
time: 468 us; the launch traced here: 465 us
  local copies, waits for them, and re-layouts  123 us (26%)
  blocking collectives  120 us (26%)
  waiting for transfers between devices  75.6 us (16%)
  matrix products  68 us (15%)
  other arithmetic  37.6 us (8%)
  starting transfers between devices  26.7 us (6%)
  between operations  14.3 us (3%)
    all_gather x1, blocking collectives, per_device(): lax.all_gather(output_weight, 'grp', axis=1, tiled=True)  111 us
    gather x14, local copies, waits for them, and re-layouts, positions_of(): starts = jnp.searchsorted(segment_ids, own_ids, side='left')  48.8 us
    all_gather x1, waiting for transfers between devices, per_device(): lax.all_gather(input_cols, 'tok', axis=0, tiled=True)  46.4 us
    dot_general x8, matrix products, one_pair(): jnp.einsum('nts,snd->tnd', weights, value_pair, preferred_element_type=jn...  33.7 us
    ppermute x6, waiting for transfers between devices, shifted(): lax.ppermute(value, axis, [(source, source + steps) for source in range(i...  29.2 us
    dot_general x8, matrix products, pair_scores(): jnp.einsum('tnd,snd->nts', query_pair, key_pair, preferred_element_type=j...  25.6 us
    slice x3, local copies, waits for them, and re-layouts, per_device(): mixed_rows = attend_pairs(queries, window[0], window[1], allowed, H)  25.3 us
    reduce_sum x8, other arithmetic, one_pair(): row_total = jnp.sum(exponent, axis=-1)  18.5 us
  transfers between devices with their start and end apart: 9, of which 2 were waited for; matrix products, arithmetic and copies ran while one was open for 42% of the time, Pallas kernels for 0%

commit v1 on v0

v1 whole, which is shorter than its diff:
```python
import functools
import math

import jax
import jax.numpy as jnp
from jax import lax
from jax.experimental import pallas as pl
from jax.experimental.pallas import tpu as pltpu
from jax.sharding import PartitionSpec as P

H = 16
SPAN = 1024
PAGE = 4

NEG_FILL = -1e30
ROPE_BASE = 160000.0
EPSILON = 1e-05
TILE = 256
CHUNK = 512
PARTS = 3
VMEM_LIMIT = 48 * 1024 * 1024


def flipped(value, axis, bit):
    count = lax.axis_size(axis)
    return lax.ppermute(value, axis, [(source, source ^ bit) for source in range(count)])


def shifted(value, axis, steps):
    count = lax.axis_size(axis)
    initial, last = (max(0, -steps), min(count, count - steps))
    return lax.ppermute(value, axis, [(source, source + steps) for source in range(initial, last)])


def flip_gather(value, axis):
    blocks = {0: value}
    bit = lax.axis_size(axis) // 2
    while bit:
        for distance in list(blocks):
            blocks[distance ^ bit] = flipped(blocks[distance], axis, bit)
        bit //= 2
    return [blocks[distance] for distance in range(lax.axis_size(axis))]


def project_kernel(group_size, peers, capacity, meta, *refs):
    tokens = refs[:group_size]
    gain, weight, cosine, sine, slots = refs[group_size : group_size + 5]
    query_out, chunk_a, chunk_b, chunk_c, send_out = refs[group_size + 5 : group_size + 10]
    normed, pairs, page_source = refs[group_size + 10 :]
    step = pl.program_id(0)
    rows = normed.shape[0]
    width = query_out.shape[1]

    for distance in range(group_size):

        @pl.when(step == distance)
        def _():
            values = tokens[distance][...].astype(jnp.float32)
            centred = values - jnp.mean(values, axis=-1, keepdims=True)
            spread = jnp.mean(jnp.square(centred), axis=-1, keepdims=True)
            normed[...] = (centred * lax.rsqrt(spread + EPSILON) * gain[...]).astype(jnp.bfloat16)

    def part(number):
        columns = pl.ds(pl.multiple_of(meta[1 + number] * width, width), width)
        return jnp.dot(normed[...], weight[:, columns], preferred_element_type=jnp.float32)

    first_half = lax.rem(lax.broadcasted_iota(jnp.int32, (rows, 128), 1), 64) < 32

    def rotate(values):
        turned = []
        for start in range(0, width, 128):
            piece = values[:, start : start + 128]
            partner = jnp.where(first_half, pltpu.roll(piece, 96, 1), pltpu.roll(piece, 32, 1))
            turned.append(piece * cosine[...] + partner * sine[...])
        return jnp.concatenate(turned, axis=1).astype(jnp.bfloat16)

    query_out[...] = rotate(part(0))
    keys = rotate(part(1))
    values = part(2).astype(jnp.bfloat16)
    block = meta[0] ^ step
    own_rows = pl.ds(pl.multiple_of(block * rows, 128), rows)
    pairs[own_rows, :width] = keys
    pairs[own_rows, width:] = values
    lane_groups = 2 * width // 128
    for lane_group in range(lane_groups):
        source = keys if lane_group < lane_groups // 2 else values
        start = lane_group % (lane_groups // 2) * 128
        page_source[lane_group] = source[:, start : start + 128].astype(jnp.float32)

    pages = rows // PAGE
    slot_count = peers * capacity
    chosen = (
        lax.broadcasted_iota(jnp.int32, (slot_count, pages), 0) == slots[0]
    ).astype(jnp.bfloat16)
    for turn in range(PAGE):
        page_part = jnp.concatenate(
            [
                page_source[lane_group, pl.ds(turn, pages, stride=PAGE), :].astype(jnp.bfloat16)
                for lane_group in range(lane_groups)
            ],
            axis=1,
        )
        placed = jnp.dot(chosen, page_part, preferred_element_type=jnp.float32)
        columns = slice(turn * 2 * width, (turn + 1) * 2 * width)
        for peer in range(peers):
            send_out[peer, 0, :, columns] = placed[
                peer * capacity : (peer + 1) * capacity
            ].astype(jnp.bfloat16)

    @pl.when(step == group_size - 1)
    def _():
        for number, chunk in enumerate((chunk_a, chunk_b, chunk_c)):
            chunk[...] = pairs[number * CHUNK : (number + 1) * CHUNK, :]


def project(meta, tokens, gain, weight, cosine, sine, slots, peers, capacity):
    group_size = len(tokens)
    rows, model_width = tokens[0].shape
    group_rows = rows * group_size
    width = weight.shape[1] // PARTS
    whole = lambda shape: pl.BlockSpec(shape, lambda i, m: (0,) * len(shape))
    block = lambda shape: pl.BlockSpec(shape, lambda i, m: (m[0] ^ i, 0))
    pages = rows // PAGE
    flops = 2 * group_rows * model_width * PARTS * width
    return pl.pallas_call(
        functools.partial(project_kernel, group_size, peers, capacity),
        grid_spec=pltpu.PrefetchScalarGridSpec(
            num_scalar_prefetch=1,
            grid=(group_size,),
            in_specs=[whole((rows, model_width))] * group_size
            + [
                whole((1, model_width)),
                whole(weight.shape),
                block((rows, 128)),
                block((rows, 128)),
                pl.BlockSpec((1, 1, pages), lambda i, m: (m[0] ^ i, 0, 0)),
            ],
            out_specs=[block((rows, width))]
            + [whole((CHUNK, 2 * width))] * 3
            + [
                pl.BlockSpec(
                    (peers, 1, capacity, 2 * PAGE * width), lambda i, m: (0, m[0] ^ i, 0, 0)
                )
            ],
            scratch_shapes=[
                pltpu.VMEM((rows, model_width), jnp.bfloat16),
                pltpu.VMEM((group_rows, 2 * width), jnp.bfloat16),
                pltpu.VMEM((2 * width // 128, rows, 128), jnp.float32),
            ],
        ),
        out_shape=[jax.ShapeDtypeStruct((group_rows, width), jnp.bfloat16)]
        + [jax.ShapeDtypeStruct((CHUNK, 2 * width), jnp.bfloat16)] * 3
        + [
            jax.ShapeDtypeStruct((peers, group_size, capacity, 2 * PAGE * width), jnp.bfloat16)
        ],
        compiler_params=pltpu.CompilerParams(vmem_limit_bytes=VMEM_LIMIT),
        cost_estimate=pl.CostEstimate(flops=flops, bytes_accessed=10 << 20, transcendentals=0),
        name="project",
    )(meta, *tokens, gain, weight, cosine, sine, slots)


def attend_kernel(head_count, meta, *refs):
    queries, starts, ends = refs[:3]
    chunks = refs[3:10]
    same_out, other_out = refs[10:12]
    pairs, masked, total, mixed, sems = refs[12:]
    step = pl.program_id(0)
    width = queries.shape[1]
    head_dim = width // head_count
    rows = same_out.shape[0]
    scale = head_dim ** (-0.5) * math.log2(math.e)

    @pl.when(step == 0)
    def _():
        copies = [
            pltpu.make_async_copy(
                chunk, pairs.at[pl.ds(number * CHUNK, CHUNK), :], sems.at[number]
            )
            for number, chunk in enumerate(chunks)
        ]
        for copy in copies:
            copy.start()
        for copy in copies:
            copy.wait()

    lane_head = lax.broadcasted_iota(jnp.int32, (TILE, width), 1) // head_dim
    for head in range(head_count):
        masked[head] = jnp.where(lane_head == head, queries[...], jnp.zeros((), jnp.bfloat16))
    total[...] = jnp.zeros_like(total)
    first, last = starts[...], ends[...]

    def visit(number, carry):
        peaks, sums = carry
        base = pl.multiple_of(number * TILE, TILE)
        keys = pairs[pl.ds(base, TILE), :width]
        values = pairs[pl.ds(base, TILE), width:].T
        index = base + lax.broadcasted_iota(jnp.int32, (TILE, TILE), 0)
        allowed = (index >= first) & (index < last)
        new_peaks, new_sums = [], []
        for head in range(head_count):
            scores = lax.dot_general(
                keys, masked[head], (((1,), (1,)), ((), ())), preferred_element_type=jnp.float32
            )
            scores = jnp.where(allowed, scores * scale, NEG_FILL)
            peak = jnp.maximum(peaks[head], jnp.max(scores, axis=0, keepdims=True))
            fade = jnp.exp2(peaks[head] - peak)
            exponent = jnp.exp2(scores - peak)
            new_peaks.append(peak)
            new_sums.append(sums[head] * fade + jnp.sum(exponent, axis=0, keepdims=True))
            dims = slice(head * head_dim, (head + 1) * head_dim)
            total[dims, :] = total[dims, :] * fade + jnp.dot(
                values[dims, :],
                exponent.astype(jnp.bfloat16),
                preferred_element_type=jnp.float32,
            )
        return tuple(new_peaks), tuple(new_sums)

    tile = meta[1] + step
    nothing = tuple(jnp.zeros((1, TILE), jnp.float32) for _ in range(head_count))
    lowest = tuple(jnp.full((1, TILE), NEG_FILL, jnp.float32) for _ in range(head_count))
    _, sums = lax.fori_loop(meta[2 + 2 * tile], meta[3 + 2 * tile], visit, (lowest, nothing))
    for head in range(head_count):
        dims = slice(head * head_dim, (head + 1) * head_dim)
        total[dims, :] = total[dims, :] / sums[head]
    mixed[pl.ds(pl.multiple_of(step * TILE, TILE), TILE), :] = total[...].T.astype(jnp.bfloat16)

    @pl.when(step == pl.num_programs(0) - 1)
    def _():
        same = meta[0]
        same_out[...] = mixed[pl.ds(pl.multiple_of(same * rows, 128), rows), :]
        other_out[...] = mixed[pl.ds(pl.multiple_of((1 - same) * rows, 128), rows), :]


def attend(meta, queries, starts, ends, chunks, rows, head_count):
    width = queries.shape[1]
    tiles = 2 * rows // TILE
    whole = pl.BlockSpec((rows, width), lambda i, m: (0, 0))
    window_rows = len(chunks) * CHUNK
    return pl.pallas_call(
        functools.partial(attend_kernel, head_count),
        grid_spec=pltpu.PrefetchScalarGridSpec(
            num_scalar_prefetch=1,
            grid=(tiles,),
            in_specs=[
                pl.BlockSpec((TILE, width), lambda i, m: (m[1] + i, 0)),
                pl.BlockSpec((1, TILE), lambda i, m: (0, m[1] + i)),
                pl.BlockSpec((1, TILE), lambda i, m: (0, m[1] + i)),
            ]
            + [pl.BlockSpec(memory_space=pl.ANY)] * len(chunks),
            out_specs=[whole, whole],
            scratch_shapes=[
                pltpu.VMEM((window_rows, 2 * width), jnp.bfloat16),
                pltpu.VMEM((head_count, TILE, width), jnp.bfloat16),
                pltpu.VMEM((width, TILE), jnp.float32),
                pltpu.VMEM((2 * rows, width), jnp.bfloat16),
                pltpu.SemaphoreType.DMA((len(chunks),)),
            ],
        ),
        out_shape=[jax.ShapeDtypeStruct((rows, width), jnp.bfloat16)] * 2,
        compiler_params=pltpu.CompilerParams(vmem_limit_bytes=VMEM_LIMIT),
        cost_estimate=pl.CostEstimate(
            flops=8 * rows * 1024 * width,
            bytes_accessed=5 << 20,
            transcendentals=2 * rows * 1024 * head_count,
        ),
        name="attend",
    )(meta, queries, starts, ends, *chunks)


def output_kernel(group_size, meta, *refs):
    mixed, weight, result = refs[:group_size], refs[group_size], refs[group_size + 1]
    width = mixed[0].shape[1]
    total = None
    for distance in range(group_size):
        depth = pl.ds(pl.multiple_of((meta[0] ^ distance) * width, width), width)
        term = jnp.dot(mixed[distance][...], weight[depth, :], preferred_element_type=jnp.float32)
        total = term if total is None else total + term
    result[...] = total.astype(jnp.bfloat16)


def output_projection(meta, mixed, weight):
    rows, width = mixed[0].shape
    depth, columns = weight.shape
    tile = min(columns, 512)
    return pl.pallas_call(
        functools.partial(output_kernel, len(mixed)),
        grid_spec=pltpu.PrefetchScalarGridSpec(
            num_scalar_prefetch=1,
            grid=(columns // tile,),
            in_specs=[pl.BlockSpec((rows, width), lambda i, m: (0, 0))] * len(mixed)
            + [pl.BlockSpec((depth, tile), lambda i, m: (0, i))],
            out_specs=pl.BlockSpec((rows, tile), lambda i, m: (0, i)),
        ),
        out_shape=jax.ShapeDtypeStruct((rows, columns), jnp.bfloat16),
        compiler_params=pltpu.CompilerParams(vmem_limit_bytes=VMEM_LIMIT),
        cost_estimate=pl.CostEstimate(
            flops=2 * rows * depth * columns, bytes_accessed=4 << 20, transcendentals=0
        ),
        name="output_projection",
    )(meta, *mixed, weight)


def unpack_kernel(group_size, received, pages):
    width = received.shape[-1] // (2 * PAGE)
    for source in range(group_size):
        for turn in range(2 * PAGE):
            start = turn * group_size * width + source * width
            pages[0, :, start : start + width] = received[
                0, source, :, turn * width : (turn + 1) * width
            ]


def unpack(received):
    peers, group_size, capacity, part = received.shape
    return pl.pallas_call(
        functools.partial(unpack_kernel, group_size),
        grid=(peers,),
        in_specs=[pl.BlockSpec((1, group_size, capacity, part), lambda i: (i, 0, 0, 0))],
        out_specs=pl.BlockSpec((1, capacity, group_size * part), lambda i: (i, 0, 0)),
        out_shape=jax.ShapeDtypeStruct((peers, capacity, group_size * part), jnp.bfloat16),
        compiler_params=pltpu.CompilerParams(vmem_limit_bytes=VMEM_LIMIT),
        cost_estimate=pl.CostEstimate(flops=0, bytes_accessed=6 << 20, transcendentals=0),
        name="unpack",
    )(received)


def rope_tables(positions):
    half_dim = 32
    inverse = 1.0 / ROPE_BASE ** (jnp.arange(half_dim, dtype=jnp.float32) * 2.0 / (2 * half_dim))
    angles = positions.astype(jnp.float32)[:, None] * jnp.tile(inverse, 4)[None, :]
    sign = jnp.where(jnp.arange(4 * half_dim) % (2 * half_dim) < half_dim, -1.0, 1.0)
    return jnp.cos(angles), jnp.sin(angles) * sign[None, :].astype(jnp.float32)


def per_device(tokens, norm_gain, input_weight, output_weight, segment_ids, page_owner):
    rows, model_width = tokens.shape
    peers, group_size = lax.axis_size("tok"), lax.axis_size("grp")
    place, member = lax.axis_index("tok"), lax.axis_index("grp")
    group_rows = rows * group_size
    width = model_width // group_size
    head_count = H // group_size
    pages = rows // PAGE

    pieces = [
        lax.ppermute(
            input_weight[:, number * width : (number + 1) * width],
            "grp",
            [(source, (PARTS * source + number) % group_size) for source in range(group_size)],
        )
        for number in range(PARTS)
    ]
    weight = lax.all_gather(jnp.concatenate(pieces, axis=1), "tok", axis=0, tiled=True)
    token_blocks = flip_gather(tokens, "grp")
    owners = lax.all_gather(page_owner[:, 0], "grp", axis=0)
    last_weight = lax.all_gather(output_weight, ("tok", "grp"), axis=0)
    last_weight = (
        last_weight.reshape((peers, group_size) + output_weight.shape)
        .transpose(0, 2, 1, 3)
        .reshape(model_width, model_width)
    )

    first_row = place * group_rows
    padded_ids = jnp.concatenate(
        [
            jnp.full((SPAN,), -1, jnp.int32),
            segment_ids,
            jnp.full((SPAN,), 1 << 30, jnp.int32),
        ]
    )
    window_ids = lax.dynamic_slice_in_dim(padded_ids, first_row, group_rows + 2 * SPAN, 0)
    own_ids = window_ids[SPAN : SPAN + group_rows]
    starts = jnp.sum((window_ids[None, :] < own_ids[:, None]).astype(jnp.int32), axis=1)
    ends = jnp.sum((window_ids[None, :] <= own_ids[:, None]).astype(jnp.int32), axis=1)
    positions = SPAN + jnp.arange(group_rows, dtype=jnp.int32) - starts
    cosine, sine = rope_tables(positions)

    capacity = max(2, (2 * pages + peers - 1) // peers)
    earlier = jnp.arange(pages)[:, None] > jnp.arange(pages)[None, :]
    same = owners[:, :, None] == owners[:, None, :]
    ranks = jnp.sum((same & earlier[None]).astype(jnp.int32), axis=2)
    slots = (owners * capacity + ranks)[:, None, :]

    order = [(number * group_size + member) % PARTS for number in range(PARTS)]
    meta = jnp.stack([member] + order).astype(jnp.int32)
    queries, chunk_a, chunk_b, chunk_c, send = project(
        meta, token_blocks, norm_gain[None, :], weight, cosine, sine, slots, peers, capacity
    )

    before_c = shifted(chunk_c, "tok", 1)
    after_a = shifted(chunk_a, "tok", -1)
    before_b = shifted(chunk_b, "tok", 1)
    after_b = shifted(chunk_b, "tok", -1)
    chunks = [before_b, before_c, chunk_a, chunk_b, chunk_c, after_a, after_b]

    received = lax.all_to_all(
        send.reshape((peers * group_size,) + send.shape[2:]),
        ("tok", "grp"),
        split_axis=0,
        concat_axis=0,
        tiled=True,
    )
    cache_pages = unpack(received.reshape(send.shape)).reshape(
        peers * capacity, 2 * PAGE * model_width
    )

    tile_first = starts[::TILE] // TILE
    tile_last = (ends[TILE - 1 :: TILE] + TILE - 1) // TILE
    ranges = jnp.stack([tile_first, tile_last], axis=1).reshape(-1)
    mixed = [None] * group_size
    for far in reversed(range(group_size // 2)):
        half = (member // 2) ^ far
        head_meta = jnp.stack([member % 2, half * (2 * rows // TILE)]).astype(jnp.int32)
        outs = attend(
            jnp.concatenate([head_meta, ranges]),
            queries,
            starts[None, :],
            ends[None, :],
            chunks,
            rows,
            head_count,
        )
        for near in range(2):
            distance = 2 * far + near
            mixed[distance] = (
                flipped(outs[near], "grp", distance) if distance else outs[near]
            )
    attended = output_projection(member[None].astype(jnp.int32), mixed, last_weight)
    return attended, cache_pages


def solution(mesh):
    placed = (
        P(("tok", "grp"), None),
        P(),
        P("tok", "grp"),
        P("tok", "grp"),
        P(),
        P(("tok", "grp"), None),
    )
    return jax.shard_map(
        per_device,
        mesh=mesh,
        in_specs=placed,
        out_specs=(P(("tok", "grp"), None), P(("tok", "grp"), None)),
        check_vma=False,
    )
```

time: 468 us -> 259 us (0.55)
  the two profiles are of different devices: /device:TPU:3 before, /device:TPU:17 now
where the time goes in v1:
time: 259 us; the launch traced here: 261 us
  waiting for transfers between devices  108 us (42%)
  Pallas kernels  63.2 us (24%)
  starting transfers between devices  37.6 us (15%)
  local copies, waits for them, and re-layouts  17.6 us (7%)
  between operations  16.4 us (6%)
  other arithmetic  10.7 us (4%)
  blocking collectives  7.06 us (3%)
    ppermute x4, waiting for transfers between devices, shifted(): lax.ppermute(value, axis, [(source, source + steps) for source in range(i...  89.7 us
    pallas_call x2, Pallas kernels, attend(): pl.pallas_call(functools.partial(attend_kernel, head_count), grid_spec=pl...  45.7 us
    ppermute x6, starting transfers between devices, flipped(): lax.ppermute(value, axis, [(source, source ^ bit) for source in range(cou...  17.3 us
    all_gather x1, waiting for transfers between devices, per_device(): lax.all_gather(jnp.concatenate(pieces, axis=1), 'tok', axis=0, tiled=True)  17 us
    unnamed x32, local copies, waits for them, and re-layouts  12.9 us
    ppermute x4, starting transfers between devices, shifted(): lax.ppermute(value, axis, [(source, source + steps) for source in range(i...  11.6 us
    pallas_call x1, Pallas kernels, project(): pl.pallas_call(functools.partial(project_kernel, group_size, peers, capac...  11.3 us
    unnamed x1, blocking collectives  7.06 us
  transfers between devices with their start and end apart: 16, of which 4 were waited for; matrix products, arithmetic and copies ran while one was open for 6% of the time, Pallas kernels for 19%

profile of v1, /device:TPU:17, one launch (start us, length us, event | category | flops | bytes accessed | tf_op | source)
XLA Modules:
  0.0 261.1 jit_solution(4335946514238991299)
XLA Ops:
  8.0 0.9 fusion.5
  9.0 3.1 %collective-permute-start.3 = (bf16[128,256]{1,0:T(8,128)(2,1)S(1)}, bf16[128,256]{1,0:T(8,128)(2,1)S(1)}, u32[]{:S(2)}, u32[]{:S(2)}) collective-permute-start(bf16[128,256]{1,0:T(8,128)(2,1)S(1)} %get-tuple-element.22), channel_id=1, source_target_pairs={{0,0},{1,3},{2,2},{3,1},{4,4},{5,7},{6,6},{7,5},{8,8},{9,11},{10,1... | collective-permute-start | bytes 196616 | tf_op jit(solution)/shard_map/ppermute | solution.py:345
  12.8 1.1 collective-permute-done.3
  14.7 1.3 collective-permute-start.1
  16.0 4.4 %collective-permute-start = (bf16[384,1024]{1,0:T(8,128)(2,1)}, bf16[384,1024]{1,0:T(8,128)(2,1)S(1)}, u32[]{:S(2)}, u32[]{:S(2)}) collective-permute-start(bf16[384,1024]{1,0:T(8,128)(2,1)} %refs_0_.1), channel_id=1, source_target_pairs={{0,1},{1,0},{2,3},{3,2},{4,5},{5,4},{6,7},{7,6},{8,9},{9,8},{10,11... | collective-permute-start | bytes 2359304 | tf_op jit(solution)/shard_map/ppermute | solution.py:26
  20.4 1.2 dynamic-slice
  23.0 7.1 %all-reduce = s32[384]{0:T(512)S(1)} all-reduce(s32[384]{0:T(512)S(1)} %bitcast_dynamic-update-slice_fusion), channel_id=2, replica_groups=mesh['tok'=8,'grp'=4] {'grp'}, use_global_device_ids=true, to_apply=%add | all-reduce | flops 384 | bytes 3072
  30.2 0.8 fusion.2
  31.4 4.4 %convert_reduce_fusion.1 = (s32[1536]{0:T(1024)S(1)}, s32[1536]{0:T(1024)S(1)}) fusion(s32[3584]{0:T(1024)S(1)} %fusion.2, s32[1536]{0:T(1024)S(1)} %slice.24), kind=kLoop, calls=%fused_computation.1 | loop fusion | flops 33027072 | bytes 32768 | tf_op jit(solution)/shard_map/reduce_sum | solution.py:372
  35.9 5.7 %collective-permute-start.2 = (bf16[384,1024]{1,0:T(8,128)(2,1)S(1)}, bf16[384,1024]{1,0:T(8,128)(2,1)S(1)}, u32[]{:S(2)}, u32[]{:S(2)}) collective-permute-start(bf16[384,1024]{1,0:T(8,128)(2,1)S(1)} %collective-permute-done.1.refs_2_), channel_id=1, source_target_pairs={{0,1},{1,0},{2,3},{3,2},{4,5},{5,4},{6,7},{7,6},{8,9},{9,8},{10,11... | collective-permute-start | bytes 2359304 | tf_op jit(solution)/shard_map/ppermute | solution.py:26
  41.7 4.3 %fusion = (f32[1536,128]{1,0:T(8,128)}, f32[1536,128]{1,0:T(8,128)}) fusion(f32[128]{0:T(128)S(1)} %compare_select_fusion, f32[128]{0:T(128)S(1)} %mul.44, f32[1536]{0:T(1024)S(1)} %subtract_convert_fusion), kind=kLoop, calls=%fused_computation.4 | loop fusion | flops 393216 | bytes 1580032 | tf_op jit(solution)/shard_map/mul | solution.py:332
  46.0 17.0 %all-gather.5.cloned.1.call-done.refs_5_ = bf16[1024,768]{1,0:T(8,128)(2,1)} async-done(((bf16[128,768]{1,0:T(8,128)(2,1)}), bf16[1024,768]{1,0:T(8,128)(2,1)}) %all-gather.5.cloned.1.call-update) | async-done | bytes 1572880 | tf_op jit(solution)/shard_map/all_gather | solution.py:352
  63.0 1.1 copy-done.2
  64.8 11.3 %project.1 = (bf16[1536,256]{1,0:T(8,128)(2,1)S(1)}, bf16[512,512]{1,0:T(8,128)(2,1)S(1)}, bf16[512,512]{1,0:T(8,128)(2,1)S(1)}, bf16[512,512]{1,0:T(8,128)(2,1)S(1)}, bf16[8,4,24,2048]{3,2,1,0:T(8,128)(2,1)}) custom-call(s32[4]{0:T(128)S(1)} %pad_add_fusion.1.meta, bf16[384,1024]{1,0:T(8,128)(2,1)S(1)} %copy-done.2, ...), custom_call_target="tpu_custom_call" | custom-call | flops 2415919104 | bytes 10485760 | tf_op jit(solution)/shard_map/project/pallas_call | solution.py:125
  78.6 0.9 copy-done.12
  79.5 4.7 %all-to-all-start = ((bf16[32,24,2048]{2,1,0:T(8,128)(2,1)}), bf16[32,24,2048]{2,1,0:T(8,128)(2,1)S(1)}, u32[]{:S(2)}, u32[]{:S(2)}) async-start(bf16[32,24,2048]{2,1,0:T(8,128)(2,1)} %bitcast.29), calls=%async_computation | async-start | bytes 6291456 | tf_op jit(solution)/shard_map/all_to_all | solution.py:395
  84.8 3.1 %collective-permute-start.6 = (bf16[512,512]{1,0:T(8,128)(2,1)}, bf16[512,512]{1,0:T(8,128)(2,1)}, u32[]{:S(2)}, u32[]{:S(2)}) collective-permute-start(bf16[512,512]{1,0:T(8,128)(2,1)} %copy-done.6), channel_id=1, source_target_pairs={{0,4},{4,8},{8,12},{12,16},{16,20},{20,24},{24,28},{1,5},{5,9},{9,... | collective-permute-start | bytes 1572872 | tf_op jit(solution)/shard_map/ppermute | solution.py:32
  87.9 3.1 %collective-permute-start.7 = (bf16[512,512]{1,0:T(8,128)(2,1)}, bf16[512,512]{1,0:T(8,128)(2,1)}, u32[]{:S(2)}, u32[]{:S(2)}) collective-permute-start(bf16[512,512]{1,0:T(8,128)(2,1)} %copy-done.9), channel_id=1, source_target_pairs={{0,4},{4,8},{8,12},{12,16},{16,20},{20,24},{24,28},{1,5},{5,9},{9,... | collective-permute-start | bytes 1572872 | tf_op jit(solution)/shard_map/ppermute | solution.py:32
  91.0 3.1 %collective-permute-start.8 = (bf16[512,512]{1,0:T(8,128)(2,1)}, bf16[512,512]{1,0:T(8,128)(2,1)}, u32[]{:S(2)}, u32[]{:S(2)}) collective-permute-start(bf16[512,512]{1,0:T(8,128)(2,1)} %copy-done.3), channel_id=1, source_target_pairs={{4,0},{8,4},{12,8},{16,12},{20,16},{24,20},{28,24},{5,1},{9,5},{13... | collective-permute-start | bytes 1572872 | tf_op jit(solution)/shard_map/ppermute | solution.py:32
  94.1 2.4 collective-permute-start.9
  97.0 78.4 %collective-permute-done.6.refs_3_ = bf16[512,512]{1,0:T(8,128)(2,1)} collective-permute-done((bf16[512,512]{1,0:T(8,128)(2,1)}, bf16[512,512]{1,0:T(8,128)(2,1)}, u32[]{:S(2)}, u32[]{:S(2)}) %collective-permute-start.6) | collective-permute-done | bytes 524320 | tf_op jit(solution)/shard_map/ppermute | solution.py:32
  175.4 11.2 %collective-permute-done.7.refs_4_ = bf16[512,512]{1,0:T(8,128)(2,1)} collective-permute-done((bf16[512,512]{1,0:T(8,128)(2,1)}, bf16[512,512]{1,0:T(8,128)(2,1)}, u32[]{:S(2)}, u32[]{:S(2)}) %collective-permute-start.7) | collective-permute-done | bytes 524320 | tf_op jit(solution)/shard_map/ppermute | solution.py:32
  186.7 1.0 copy-done.4
  187.7 1.0 copy-done.7
  188.8 1.0 copy-done.10
  189.8 1.1 copy-done.13
  190.9 21.2 %attend.3 = (bf16[384,256]{1,0:T(8,128)(2,1)}, bf16[384,256]{1,0:T(8,128)(2,1)}) custom-call(s32[14]{0:T(128)S(1)} %get-tuple-element.27.meta, bf16[1536,256]{1,0:T(8,128)(2,1)S(1)} %copy-done.13, s32[1,1536]{1,0:T(1,128)S(1)} %broadcast_in_dim.49.refs_1_, s32[1,1536]{1,0:T(1,128)S(1)} %broadcast_in_dim.50.refs_2_, ...), custom_call_target="tpu_custom_call" | custom-call | flops 805306368 | bytes 5242880 | tf_op jit(solution)/shard_map/attend/pallas_call | solution.py:239
  212.2 5.2 %collective-permute-start.11 = (bf16[384,256]{1,0:T(8,128)(2,1)}, bf16[384,256]{1,0:T(8,128)(2,1)S(1)}, u32[]{:S(2)}, u32[]{:S(2)}) collective-permute-start(bf16[384,256]{1,0:T(8,128)(2,1)} %get-tuple-element.17), channel_id=1, source_target_pairs={{0,2},{1,3},{2,0},{3,1},{4,6},{5,7},{6,4},{7,5},{8,10},{9,11},{10,... | collective-permute-start | bytes 589832 | tf_op jit(solution)/shard_map/ppermute | solution.py:26
  217.8 24.5 %attend.2 = (bf16[384,256]{1,0:T(8,128)(2,1)S(1)}, bf16[384,256]{1,0:T(8,128)(2,1)}) custom-call(s32[14]{0:T(128)S(1)} %get-tuple-element.28.meta, bf16[1536,256]{1,0:T(8,128)(2,1)S(1)} %copy-done.13, s32[1,1536]{1,0:T(1,128)S(1)} %broadcast_in_dim.49.refs_1_, s32[1,1536]{1,0:T(1,128)S(1)} %broadcast_in_dim.50.refs_2_, ...), custom_call_target="tpu_custom_call" | custom-call | flops 805306368 | bytes 5242880 | tf_op jit(solution)/shard_map/attend/pallas_call | solution.py:239
  243.3 3.2 %copy.13 = bf16[8,4,128,256]{3,1,2,0:T(4,128)(2,1)S(1)} copy(bf16[8,4,128,256]{3,2,1,0:T(8,128)(2,1)} %bitcast.31) | data formatting | bytes 4194304 | tf_op jit(solution)/shard_map/reshape | solution.py:357
  247.4 2.9 %output_projection.1 = bf16[384,1024]{1,0:T(8,128)(2,1)} custom-call(s32[1]{0:T(128)} %bitcast.meta, bf16[384,256]{1,0:T(8,128)(2,1)S(1)} %copy-done.1, bf16[384,256]{1,0:T(8,128)(2,1)} %collective-permute-done.10.refs_1_, bf16[384,256]{1,0:T(8,128)(2,1)S(1)} %collective-permute-done.11.refs_2_, bf16[384,256]{1,0:T(8,128)(2,1)S(1)} %collective-permute-done.12.refs_3_, ...), custom_call_target="tpu_custom_call" | custom-call | flops 805306368 | bytes 4194304 | tf_op jit(solution)/shard_map/output_projection/pallas_call | solution.py:285
  250.3 3.3 %unpack.1 = bf16[8,24,8192]{2,1,0:T(8,128)(2,1)} custom-call(bf16[8,4,24,2048]{3,2,1,0:T(8,128)(2,1)S(1)} %bitcast.24), custom_call_target="tpu_custom_call" | custom-call | bytes 6291456 | tf_op jit(solution)/shard_map/unpack/pallas_call | solution.py:315
  (68 shorter events, 9.2 us)
Async XLA Ops:
  8.0 55.0 %all-gather.5.cloned.1.call-start = ((), (), s32[]{:S(2)}) async-start(), calls=%async_computation.1 | async-start | bytes 1769472 | tf_op jit(solution)/shard_map/all_gather | solution.py:352
  9.0 5.0 %collective-permute-start.3 = (bf16[128,256]{1,0:T(8,128)(2,1)S(1)}, bf16[128,256]{1,0:T(8,128)(2,1)S(1)}, u32[]{:S(2)}, u32[]{:S(2)}) collective-permute-start(bf16[128,256]{1,0:T(8,128)(2,1)S(1)} %get-tuple-element.22), channel_id=1, source_target_pairs={{0,0},{1,3},{2,2},{3,1},{4,4},{5,7},{6,6},{7,5},{8,8},{9,11},{10,1... | collective-permute-start | bytes 196616 | tf_op jit(solution)/shard_map/ppermute | solution.py:345
  12.1 1.9 collective-permute-start.4
  12.2 1.8 collective-permute-start.5
  14.7 21.2 %collective-permute-start.1 = (bf16[384,1024]{1,0:T(8,128)(2,1)}, bf16[384,1024]{1,0:T(8,128)(2,1)S(1)}, u32[]{:S(2)}, u32[]{:S(2)}) collective-permute-start(bf16[384,1024]{1,0:T(8,128)(2,1)} %refs_0_.1), channel_id=1, source_target_pairs={{0,2},{1,3},{2,0},{3,1},{4,6},{5,7},{6,4},{7,5},{8,10},{9,11},{10,... | collective-permute-start | bytes 2359304 | tf_op jit(solution)/shard_map/ppermute | solution.py:26
  16.0 30.0 %collective-permute-start = (bf16[384,1024]{1,0:T(8,128)(2,1)}, bf16[384,1024]{1,0:T(8,128)(2,1)S(1)}, u32[]{:S(2)}, u32[]{:S(2)}) collective-permute-start(bf16[384,1024]{1,0:T(8,128)(2,1)} %refs_0_.1), channel_id=1, source_target_pairs={{0,1},{1,0},{2,3},{3,2},{4,5},{5,4},{6,7},{7,6},{8,9},{9,8},{10,11... | collective-permute-start | bytes 2359304 | tf_op jit(solution)/shard_map/ppermute | solution.py:26
  35.9 10.1 %collective-permute-start.2 = (bf16[384,1024]{1,0:T(8,128)(2,1)S(1)}, bf16[384,1024]{1,0:T(8,128)(2,1)S(1)}, u32[]{:S(2)}, u32[]{:S(2)}) collective-permute-start(bf16[384,1024]{1,0:T(8,128)(2,1)S(1)} %collective-permute-done.1.refs_2_), channel_id=1, source_target_pairs={{0,1},{1,0},{2,3},{3,2},{4,5},{5,4},{6,7},{7,6},{8,9},{9,8},{10,11... | collective-permute-start | bytes 2359304 | tf_op jit(solution)/shard_map/ppermute | solution.py:26
  63.0 1.1 copy-start.2
  64.2 0.7 copy-start.11
  76.2 0.8 copy-start.3
  77.0 0.8 copy-start.6
  77.8 0.8 copy-start.9
  78.6 0.9 copy-start.12
  79.5 170.8 %all-to-all-start = ((bf16[32,24,2048]{2,1,0:T(8,128)(2,1)}), bf16[32,24,2048]{2,1,0:T(8,128)(2,1)S(1)}, u32[]{:S(2)}, u32[]{:S(2)}) async-start(bf16[32,24,2048]{2,1,0:T(8,128)(2,1)} %bitcast.29), calls=%async_computation | async-start | bytes 6291456 | tf_op jit(solution)/shard_map/all_to_all | solution.py:395
  84.2 159.0 %all-gather.7.cloned.1.call-start = ((), (), s32[]{:S(2)}) async-start(), calls=%async_computation.2 | async-start | bytes 2162688 | tf_op jit(solution)/shard_map/all_gather | solution.py:355
  84.8 90.6 %collective-permute-start.6 = (bf16[512,512]{1,0:T(8,128)(2,1)}, bf16[512,512]{1,0:T(8,128)(2,1)}, u32[]{:S(2)}, u32[]{:S(2)}) collective-permute-start(bf16[512,512]{1,0:T(8,128)(2,1)} %copy-done.6), channel_id=1, source_target_pairs={{0,4},{4,8},{8,12},{12,16},{16,20},{20,24},{24,28},{1,5},{5,9},{9,... | collective-permute-start | bytes 1572872 | tf_op jit(solution)/shard_map/ppermute | solution.py:32
  87.9 98.8 %collective-permute-start.7 = (bf16[512,512]{1,0:T(8,128)(2,1)}, bf16[512,512]{1,0:T(8,128)(2,1)}, u32[]{:S(2)}, u32[]{:S(2)}) collective-permute-start(bf16[512,512]{1,0:T(8,128)(2,1)} %copy-done.9), channel_id=1, source_target_pairs={{0,4},{4,8},{8,12},{12,16},{16,20},{20,24},{24,28},{1,5},{5,9},{9,... | collective-permute-start | bytes 1572872 | tf_op jit(solution)/shard_map/ppermute | solution.py:32
  91.0 95.6 %collective-permute-start.8 = (bf16[512,512]{1,0:T(8,128)(2,1)}, bf16[512,512]{1,0:T(8,128)(2,1)}, u32[]{:S(2)}, u32[]{:S(2)}) collective-permute-start(bf16[512,512]{1,0:T(8,128)(2,1)} %copy-done.3), channel_id=1, source_target_pairs={{4,0},{8,4},{12,8},{16,12},{20,16},{24,20},{28,24},{5,1},{9,5},{13... | collective-permute-start | bytes 1572872 | tf_op jit(solution)/shard_map/ppermute | solution.py:32
  94.1 92.6 %collective-permute-start.9 = (bf16[512,512]{1,0:T(8,128)(2,1)}, bf16[512,512]{1,0:T(8,128)(2,1)}, u32[]{:S(2)}, u32[]{:S(2)}) collective-permute-start(bf16[512,512]{1,0:T(8,128)(2,1)} %copy-done.6), channel_id=1, source_target_pairs={{4,0},{8,4},{12,8},{16,12},{20,16},{24,20},{28,24},{5,1},{9,5},{13... | collective-permute-start | bytes 1572872 | tf_op jit(solution)/shard_map/ppermute | solution.py:32
  186.7 1.0 copy-start.4
  187.7 1.0 copy-start.7
  188.8 1.0 copy-start.10
  189.8 1.1 copy-start.13
  190.9 26.8 %copy-start.5 = (bf16[512,512]{1,0:T(8,128)(2,1)S(1)}, bf16[512,512]{1,0:T(8,128)(2,1)}, u32[]{:S(2)}) copy-start(bf16[512,512]{1,0:T(8,128)(2,1)} %copy-done.3) | copy-start | bytes 1572868
  190.9 26.8 %copy-start.8 = (bf16[512,512]{1,0:T(8,128)(2,1)S(1)}, bf16[512,512]{1,0:T(8,128)(2,1)}, u32[]{:S(2)}) copy-start(bf16[512,512]{1,0:T(8,128)(2,1)} %copy-done.6) | copy-start | bytes 1572868
  212.2 34.8 %collective-permute-start.11 = (bf16[384,256]{1,0:T(8,128)(2,1)}, bf16[384,256]{1,0:T(8,128)(2,1)S(1)}, u32[]{:S(2)}, u32[]{:S(2)}) collective-permute-start(bf16[384,256]{1,0:T(8,128)(2,1)} %get-tuple-element.17), channel_id=1, source_target_pairs={{0,2},{1,3},{2,0},{3,1},{4,6},{5,7},{6,4},{7,5},{8,10},{9,11},{10,... | collective-permute-start | bytes 589832 | tf_op jit(solution)/shard_map/ppermute | solution.py:26
  217.4 29.6 %collective-permute-start.12 = (bf16[384,256]{1,0:T(8,128)(2,1)}, bf16[384,256]{1,0:T(8,128)(2,1)S(1)}, u32[]{:S(2)}, u32[]{:S(2)}) collective-permute-start(bf16[384,256]{1,0:T(8,128)(2,1)} %get-tuple-element.18), channel_id=1, source_target_pairs={{0,3},{1,2},{2,1},{3,0},{4,7},{5,6},{6,5},{7,4},{8,11},{9,10},{10,... | collective-permute-start | bytes 589832 | tf_op jit(solution)/shard_map/ppermute | solution.py:26
  242.2 0.7 copy-start
  242.9 4.1 %collective-permute-start.10 = (bf16[384,256]{1,0:T(8,128)(2,1)}, bf16[384,256]{1,0:T(8,128)(2,1)}, u32[]{:S(2)}, u32[]{:S(2)}) collective-permute-start(bf16[384,256]{1,0:T(8,128)(2,1)} %get-tuple-element.16), channel_id=1, source_target_pairs={{0,1},{1,0},{2,3},{3,2},{4,5},{5,4},{6,7},{7,6},{8,9},{9,8},{10,11... | collective-permute-start | bytes 589832 | tf_op jit(solution)/shard_map/ppermute | solution.py:26
  246.5 0.9 copy-start.1
Sparse Core Ops, SparseCore 0:
  14.8 48.1 all-gather.4
Sparse Core Ops, SparseCore 1:
  87.6 84.7 all-gather.6

commit v2 on v0

v2 whole, which is shorter than its diff:
```python
import functools
import math

import jax
import jax.numpy as jnp
from jax import lax
from jax.experimental import pallas as pl
from jax.experimental.pallas import tpu as pltpu
from jax.sharding import PartitionSpec as P

H = 16
SPAN = 1024
PAGE = 4
HEAD_DIM = 64

NEG_FILL = -1e30
ROPE_BASE = 160000.0
EPSILON = 1e-05
TILE = 256
PARTS = 3
PAIR = 2
ONES_ROWS = 16
HEAD_ROWS = HEAD_DIM + ONES_ROWS
VMEM_LIMIT = 60 * 1024 * 1024
PARAMS = pltpu.CompilerParams(vmem_limit_bytes=VMEM_LIMIT)


def flipped(value, axis, bit):
    count = lax.axis_size(axis)
    return lax.ppermute(value, axis, [(source, source ^ bit) for source in range(count)])


def shifted(value, axis, steps):
    count = lax.axis_size(axis)
    initial, last = (max(0, -steps), min(count, count - steps))
    return lax.ppermute(value, axis, [(source, source + steps) for source in range(initial, last)])


def norm_kernel(tokens, gain, normed):
    values = tokens[...].astype(jnp.float32)
    centred = values - jnp.mean(values, axis=-1, keepdims=True)
    spread = jnp.mean(jnp.square(centred), axis=-1, keepdims=True)
    normed[...] = (centred * lax.rsqrt(spread + EPSILON) * gain[...]).astype(jnp.bfloat16)


def layer_norm(tokens, gain):
    rows, width = tokens.shape
    tile = rows // 3
    return pl.pallas_call(
        norm_kernel,
        grid=(3,),
        in_specs=[
            pl.BlockSpec((tile, width), lambda i: (i, 0)),
            pl.BlockSpec((1, width), lambda i: (0, 0)),
        ],
        out_specs=pl.BlockSpec((tile, width), lambda i: (i, 0)),
        out_shape=jax.ShapeDtypeStruct(tokens.shape, jnp.bfloat16),
        compiler_params=PARAMS,
        name="layer_norm",
    )(tokens, gain)


def project_kernel(layout, weight_count, peers, capacity, meta, *refs):
    operands = 1 + max(entry[0] for pieces in layout for entry in pieces)
    tokens = refs[:operands]
    weights = refs[operands : operands + weight_count]
    cosine, sine, slots, query_out, chunk_a, chunk_b, chunk_c, send_out = refs[
        operands + weight_count : operands + weight_count + 8
    ]
    blocks, weight, pairs, page_source, sems = refs[operands + weight_count + 8 :]
    step = pl.program_id(0)
    steps = len(layout)
    rows = blocks.shape[1]
    width = query_out.shape[1]
    shard = weights[0].shape[0] // 2

    def arrivals(distance):
        return [
            pltpu.make_async_copy(
                tokens[operand],
                blocks.at[distance, pl.ds(offset, count), :],
                sems.at[distance, number],
            )
            for number, (operand, offset, count) in enumerate(layout[distance])
        ]

    @pl.when(step == 0)
    def _():
        for distance in range(steps):
            for copy in arrivals(distance):
                copy.start()
        for plane in range(weight_count):
            for low in range(2):
                row = pl.multiple_of((meta[1] ^ (2 * plane + low)) * shard, shard)
                for number in range(PARTS):
                    column = pl.multiple_of(meta[2 + number] * width, width)
                    weight[pl.ds(row, shard), number * width : (number + 1) * width] = weights[
                        plane
                    ][low * shard : (low + 1) * shard, pl.ds(column, width)]

    for distance in range(steps):

        @pl.when(step == distance)
        def _():
            for copy in arrivals(distance):
                copy.wait()

    joined = jnp.dot(blocks[step], weight[...], preferred_element_type=jnp.float32)
    cosines = jnp.concatenate([cosine[...]] * 4, axis=0).T
    sines = jnp.concatenate([-sine[...], sine[...]] * 2, axis=0).T
    first_half = lax.rem(lax.broadcasted_iota(jnp.int32, (rows, width), 1), HEAD_DIM) < (
        HEAD_DIM // 2
    )

    def rotate(values):
        partner = jnp.where(
            first_half,
            pltpu.roll(values, width - HEAD_DIM // 2, 1),
            pltpu.roll(values, HEAD_DIM // 2, 1),
        )
        return values * cosines + partner * sines

    scale = HEAD_DIM ** (-0.5) * math.log2(math.e)
    query_out[...] = (rotate(joined[:, :width]) * scale).astype(jnp.bfloat16)
    keys = rotate(joined[:, width : 2 * width]).astype(jnp.bfloat16)
    values = joined[:, 2 * width :].astype(jnp.bfloat16)
    block = meta[0] ^ step
    own_rows = pl.ds(pl.multiple_of(block * rows, 128), rows)
    pairs[own_rows, :width] = keys
    pairs[own_rows, width:] = values
    page_source[0] = keys.astype(jnp.float32)
    page_source[1] = values.astype(jnp.float32)

    pages = rows // PAGE
    slot_count = peers * capacity
    chosen = (
        lax.broadcasted_iota(jnp.int32, (slot_count, pages), 0) == slots[0]
    ).astype(jnp.bfloat16)
    for turn in range(PAGE):
        page_part = jnp.concatenate(
            [
                page_source[half, pl.ds(turn, pages, stride=PAGE), :].astype(jnp.bfloat16)
                for half in range(2)
            ],
            axis=1,
        )
        placed = jnp.dot(chosen, page_part, preferred_element_type=jnp.float32)
        columns = slice(turn * 2 * width, (turn + 1) * 2 * width)
        for peer in range(peers):
            send_out[peer, 0, 0, :, columns] = placed[
                peer * capacity : (peer + 1) * capacity
            ].astype(jnp.bfloat16)

    @pl.when(step == steps - 1)
    def _():
        for number, chunk in enumerate((chunk_a, chunk_b, chunk_c)):
            chunk[...] = pairs[number * SPAN : (number + 1) * SPAN, :]


def project(meta, layout, operands, weights, cosine, sine, slots, rows, peers, capacity):
    steps = len(layout)
    model_width = operands[0].shape[1]
    group_rows = rows * steps
    width = weights[0].shape[1] // PARTS
    pages = rows // PAGE
    members = steps // PAIR
    whole = lambda shape: pl.BlockSpec(shape, lambda i, m: (0,) * len(shape))
    table = pl.BlockSpec((HEAD_DIM // 2, rows), lambda i, m: (0, m[0] ^ i))
    send_shape = (peers, members, PAIR, capacity, 2 * PAGE * width)
    return pl.pallas_call(
        functools.partial(project_kernel, layout, len(weights), peers, capacity),
        grid_spec=pltpu.PrefetchScalarGridSpec(
            num_scalar_prefetch=1,
            grid=(steps,),
            in_specs=[pl.BlockSpec(memory_space=pl.ANY)] * len(operands)
            + [whole(weights[0].shape)] * len(weights)
            + [table, table, pl.BlockSpec((1, 1, pages), lambda i, m: (m[0] ^ i, 0, 0))],
            out_specs=[pl.BlockSpec((rows, width), lambda i, m: (m[0] ^ i, 0))]
            + [whole((SPAN, 2 * width))] * 3
            + [
                pl.BlockSpec(
                    (peers, 1, 1) + send_shape[3:],
                    lambda i, m: (0, (m[0] ^ i) % members, (m[0] ^ i) // members, 0, 0),
                )
            ],
            scratch_shapes=[
                pltpu.VMEM((steps, rows, model_width), jnp.bfloat16),
                pltpu.VMEM((model_width, PARTS * width), jnp.bfloat16),
                pltpu.VMEM((group_rows, 2 * width), jnp.bfloat16),
                pltpu.VMEM((2, rows, width), jnp.float32),
                pltpu.SemaphoreType.DMA((steps, 2)),
            ],
        ),
        out_shape=[jax.ShapeDtypeStruct((group_rows, width), jnp.bfloat16)]
        + [jax.ShapeDtypeStruct((SPAN, 2 * width), jnp.bfloat16)] * 3
        + [jax.ShapeDtypeStruct(send_shape, jnp.bfloat16)],
        compiler_params=PARAMS,
        cost_estimate=pl.CostEstimate(
            flops=2 * group_rows * model_width * PARTS * width,
            bytes_accessed=12 << 20,
            transcendentals=0,
        ),
        name="project",
    )(meta, *operands, *weights, cosine, sine, slots)


def mask_heads(queries, masked):
    head_of_lane = lax.broadcasted_iota(jnp.int32, queries.shape, 1) // HEAD_DIM
    for head in range(masked.shape[0]):
        masked[head] = jnp.where(head_of_lane == head, queries[...], jnp.zeros((), jnp.bfloat16))


def with_ones(values):
    turned = values.T
    ones = jnp.ones((ONES_ROWS, values.shape[0]), values.dtype)
    rows = []
    for head in range(values.shape[1] // HEAD_DIM):
        rows += [turned[head * HEAD_DIM : (head + 1) * HEAD_DIM], ones]
    return jnp.concatenate(rows, axis=0)


def visit(keys, values, first_key, masked, starts, ends, total, peaks):
    index = first_key + lax.broadcasted_iota(jnp.int32, (TILE, TILE), 0)
    allowed = (index >= starts) & (index < ends)
    new_peaks = []
    for head, old_peak in enumerate(peaks):
        scores = lax.dot_general(
            keys, masked[head], (((1,), (1,)), ((), ())), preferred_element_type=jnp.float32
        )
        scores = jnp.where(allowed, scores, NEG_FILL)
        peak = jnp.maximum(old_peak, jnp.max(scores, axis=0, keepdims=True))
        fade = jnp.exp2(old_peak - peak)
        weights = jnp.exp2(scores - peak).astype(jnp.bfloat16)
        own = slice(head * HEAD_ROWS, (head + 1) * HEAD_ROWS)
        total[own, :] = total[own, :] * fade + jnp.dot(
            values[own, :], weights, preferred_element_type=jnp.float32
        )
        new_peaks.append(peak)
    return tuple(new_peaks)


def attend_kernel(ranges, queries, starts, ends, chunk_a, chunk_b, chunk_c, total, peak_out, *scratch):
    masked, values = scratch
    step = pl.program_id(0)
    width = queries.shape[1]
    heads = width // HEAD_DIM
    per_chunk = SPAN // TILE
    chunks = (chunk_a, chunk_b, chunk_c)

    @pl.when(step == 0)
    def _():
        for number in range(len(chunks) * per_chunk):
            rows = slice(number % per_chunk * TILE, (number % per_chunk + 1) * TILE)
            values[number] = with_ones(chunks[number // per_chunk][rows, width:])

    mask_heads(queries, masked)
    total[...] = jnp.zeros_like(total)
    first, last = starts[...], ends[...]
    peaks = tuple(jnp.full((1, TILE), NEG_FILL, jnp.float32) for _ in range(heads))
    for number, chunk in enumerate(chunks):
        base = (number + 1) * per_chunk

        def one(block, peaks):
            rows = pl.ds(pl.multiple_of((block - base) * TILE, TILE), TILE)
            return visit(
                chunk[rows, :width],
                values[block - per_chunk],
                block * TILE,
                masked,
                first,
                last,
                total.at[0],
                peaks,
            )

        begin = jnp.maximum(ranges[2 * step], base)
        peaks = lax.fori_loop(
            begin, jnp.minimum(ranges[2 * step + 1], base + per_chunk), one, peaks
        )
    for head in range(heads):
        peak_out[0, head : head + 1, :] = peaks[head]


def finish_kernel(meta, queries, starts, ends, before, after, total, peak_in, *refs):
    outs = refs[:-3]
    masked, sums, mixed = refs[-3:]
    step = pl.program_id(0)
    width = queries.shape[1]
    heads = width // HEAD_DIM
    per_chunk = SPAN // TILE
    own_blocks = pl.num_programs(0)
    sums[...] = total[0]
    begin, end = meta[1 + 2 * step], meta[2 + 2 * step]

    @pl.when((begin < per_chunk) | (end > per_chunk + own_blocks))
    def _():
        mask_heads(queries, masked)
        first, last = starts[...], ends[...]
        peaks = tuple(peak_in[0, head : head + 1, :] for head in range(heads))
        for chunk, base in ((before, 0), (after, per_chunk + own_blocks)):

            def one(block, peaks):
                rows = pl.ds(pl.multiple_of((block - base) * TILE, TILE), TILE)
                return visit(
                    chunk[rows, :width],
                    with_ones(chunk[rows, width:]),
                    block * TILE,
                    masked,
                    first,
                    last,
                    sums,
                    peaks,
                )

            peaks = lax.fori_loop(
                jnp.maximum(begin, base), jnp.minimum(end, base + per_chunk), one, peaks
            )

    parts = []
    for head in range(heads):
        row = head * HEAD_ROWS
        parts.append(sums[row : row + HEAD_DIM, :] / sums[row + HEAD_DIM : row + HEAD_DIM + 1, :])
    tile_rows = pl.ds(pl.multiple_of(step * TILE, TILE), TILE)
    mixed[tile_rows, :] = jnp.concatenate(parts, axis=0).T.astype(jnp.bfloat16)

    @pl.when(step == pl.num_programs(0) - 1)
    def _():
        rows = outs[0].shape[0]
        for distance, out in enumerate(outs):
            out[...] = mixed[pl.ds(pl.multiple_of((meta[0] ^ distance) * rows, 128), rows), :]


def attend_specs(width, prefetched):
    spec = lambda shape, index: pl.BlockSpec(shape, lambda i, m: index(i))
    return [
        spec((TILE, width), lambda i: (i, 0)),
        spec((1, TILE), lambda i: (0, i)),
        spec((1, TILE), lambda i: (0, i)),
    ] + [spec((SPAN, 2 * width), lambda i: (0, 0))] * prefetched


def attend_local(ranges, queries, starts, ends, chunks):
    group_rows, width = queries.shape
    heads = width // HEAD_DIM
    tiles = group_rows // TILE
    blocks = len(chunks) * SPAN // TILE
    return pl.pallas_call(
        attend_kernel,
        grid_spec=pltpu.PrefetchScalarGridSpec(
            num_scalar_prefetch=1,
            grid=(tiles,),
            in_specs=attend_specs(width, len(chunks)),
            out_specs=[
                pl.BlockSpec((1, heads * HEAD_ROWS, TILE), lambda i, m: (i, 0, 0)),
                pl.BlockSpec((1, 8, TILE), lambda i, m: (i, 0, 0)),
            ],
            scratch_shapes=[
                pltpu.VMEM((heads, TILE, width), jnp.bfloat16),
                pltpu.VMEM((blocks, heads * HEAD_ROWS, TILE), jnp.bfloat16),
            ],
        ),
        out_shape=[
            jax.ShapeDtypeStruct((tiles, heads * HEAD_ROWS, TILE), jnp.float32),
            jax.ShapeDtypeStruct((tiles, 8, TILE), jnp.float32),
        ],
        compiler_params=PARAMS,
        cost_estimate=pl.CostEstimate(
            flops=16 * group_rows * 1024 * width,
            bytes_accessed=5 << 20,
            transcendentals=group_rows * 1024 * heads,
        ),
        name="attend_local",
    )(ranges, queries, starts, ends, *chunks)


def attend_finish(meta, queries, starts, ends, before, after, total, peaks, rows):
    group_rows, width = queries.shape
    heads = width // HEAD_DIM
    tiles = group_rows // TILE
    members = group_rows // rows
    return pl.pallas_call(
        finish_kernel,
        grid_spec=pltpu.PrefetchScalarGridSpec(
            num_scalar_prefetch=1,
            grid=(tiles,),
            in_specs=attend_specs(width, 2)
            + [
                pl.BlockSpec((1,) + total.shape[1:], lambda i, m: (i, 0, 0)),
                pl.BlockSpec((1,) + peaks.shape[1:], lambda i, m: (i, 0, 0)),
            ],
            out_specs=[pl.BlockSpec((rows, width), lambda i, m: (0, 0))] * members,
            scratch_shapes=[
                pltpu.VMEM((heads, TILE, width), jnp.bfloat16),
                pltpu.VMEM(total.shape[1:], jnp.float32),
                pltpu.VMEM((group_rows, width), jnp.bfloat16),
            ],
        ),
        out_shape=[jax.ShapeDtypeStruct((rows, width), jnp.bfloat16)] * members,
        compiler_params=PARAMS,
        cost_estimate=pl.CostEstimate(
            flops=4 * group_rows * 1024 * width,
            bytes_accessed=5 << 20,
            transcendentals=group_rows * 256 * heads,
        ),
        name="attend_finish",
    )(meta, queries, starts, ends, before, after, total, peaks)


def output_kernel(members, meta, *refs):
    parts, weight, result, mixed = refs[:members], refs[members], refs[-2], refs[-1]
    width = parts[0].shape[1]

    @pl.when(pl.program_id(0) == 0)
    def _():
        for distance in range(members):
            source = meta[0] ^ distance
            head_pair = PAIR * (source % (members // PAIR)) + source // (members // PAIR)
            columns = pl.ds(pl.multiple_of(head_pair * width, width), width)
            mixed[:, columns] = parts[distance][...]

    result[...] = jnp.dot(
        mixed[...], weight[...], preferred_element_type=jnp.float32
    ).astype(jnp.bfloat16)


def output_projection(meta, parts, weight):
    rows, width = parts[0].shape
    depth = width * len(parts)
    tile = weight.shape[1]
    steps = weight.shape[0] // depth
    return pl.pallas_call(
        functools.partial(output_kernel, len(parts)),
        grid_spec=pltpu.PrefetchScalarGridSpec(
            num_scalar_prefetch=1,
            grid=(steps,),
            in_specs=[pl.BlockSpec((rows, width), lambda i, m: (0, 0))] * len(parts)
            + [pl.BlockSpec((depth, tile), lambda i, m: (i, 0))],
            out_specs=pl.BlockSpec((rows, tile), lambda i, m: (0, i)),
            scratch_shapes=[pltpu.VMEM((rows, depth), jnp.bfloat16)],
        ),
        out_shape=jax.ShapeDtypeStruct((rows, steps * tile), jnp.bfloat16),
        compiler_params=PARAMS,
        cost_estimate=pl.CostEstimate(
            flops=2 * rows * depth * steps * tile, bytes_accessed=4 << 20, transcendentals=0
        ),
        name="output_projection",
    )(meta, *parts, weight)


def unpack_kernel(received, pages):
    _, pair, members, _, capacity, part = received.shape
    width = part // (2 * PAGE)
    for low in range(pair):
        for high in range(members):
            head_pair = PAIR * high + low
            for turn in range(2 * PAGE):
                start = (turn * pair * members + head_pair) * width
                pages[0, :, start : start + width] = received[
                    0, low, high, 0, :, turn * width : (turn + 1) * width
                ]


def unpack(received):
    planes, pair, members, sources, capacity, part = received.shape
    return pl.pallas_call(
        unpack_kernel,
        grid=(planes, sources),
        in_specs=[
            pl.BlockSpec(
                (1, pair, members, 1, capacity, part), lambda i, j: (i, 0, 0, j, 0, 0)
            )
        ],
        out_specs=pl.BlockSpec(
            (1, capacity, pair * members * part), lambda i, j: (i * sources + j, 0, 0)
        ),
        out_shape=jax.ShapeDtypeStruct(
            (planes * sources, capacity, pair * members * part), jnp.bfloat16
        ),
        compiler_params=PARAMS,
        cost_estimate=pl.CostEstimate(flops=0, bytes_accessed=6 << 20, transcendentals=0),
        name="unpack",
    )(received)


def rope_tables(positions):
    half_dim = HEAD_DIM // 2
    inverse = 1.0 / ROPE_BASE ** (jnp.arange(half_dim, dtype=jnp.float32) * 2.0 / HEAD_DIM)
    angles = inverse[:, None] * positions.astype(jnp.float32)[None, :]
    return jnp.cos(angles), jnp.sin(angles)


def document_bounds(window_ids, rows, blocks):
    reach = SPAN + rows
    firsts = jnp.arange(blocks, dtype=jnp.int32)[:, None] * rows
    own = window_ids[SPAN : SPAN + rows * blocks].reshape(blocks, rows)
    behind = jnp.stack([window_ids[k * rows : k * rows + reach] for k in range(blocks)])
    ahead = jnp.stack(
        [window_ids[SPAN + k * rows : SPAN + k * rows + reach] for k in range(blocks)]
    )
    starts = jnp.sum((behind[:, None, :] < own[:, :, None]).astype(jnp.int32), axis=2) + firsts
    ends = (
        jnp.sum((ahead[:, None, :] <= own[:, :, None]).astype(jnp.int32), axis=2)
        + firsts
        + SPAN
    )
    return starts.reshape(-1), ends.reshape(-1)


def per_device(tokens, norm_gain, input_weight, output_weight, segment_ids, page_owner):
    rows, model_width = tokens.shape
    peers, members = lax.axis_size("tok"), lax.axis_size("grp")
    place, column = lax.axis_index("tok"), lax.axis_index("grp")
    low = place % PAIR
    blocks = PAIR * members
    member = low * members + column
    group_rows = rows * blocks
    width = model_width // blocks
    pages = rows // PAGE

    shard = input_weight.reshape(input_weight.shape[0], PARTS, PAIR, width)
    mine = lax.dynamic_index_in_dim(shard, low, 2, keepdims=False)
    theirs = lax.dynamic_index_in_dim(shard, 1 - low, 2, keepdims=False)
    both = jnp.concatenate([mine, flipped(theirs, "tok", 1)], axis=0)
    pieces = [
        lax.ppermute(
            both[:, number],
            "grp",
            [(source, (PARTS * source + number) % members) for source in range(members)],
        )
        for number in range(PARTS)
    ]
    planes = {0: jnp.concatenate(pieces, axis=1)}
    bit = peers // 2
    while bit > 1:
        for distance in list(planes):
            planes[distance ^ bit] = flipped(planes[distance], "tok", bit)
        bit //= 2
    weights = [planes[distance] for distance in range(0, peers, 2)]

    own = layer_norm(tokens, norm_gain[None, :])
    across, along = flipped(own, "grp", 2), flipped(own, "tok", 1)
    half = rows // 2
    corner_top = flipped(across[:half], "tok", 1)
    corner_bottom = flipped(along[half:], "grp", 2)
    operands = [own, across, along, corner_top, corner_bottom]
    operands += [flipped(operand, "grp", 1) for operand in operands]
    layout = [None] * blocks
    for near in range(2):
        shift = 5 * near
        layout[near] = [(shift, 0, rows)]
        layout[2 + near] = [(shift + 1, 0, rows)]
        layout[4 + near] = [(shift + 2, 0, rows)]
        layout[6 + near] = [(shift + 3, 0, half), (shift + 4, half, half)]

    owners = page_owner[:, 0]
    capacity = max(2, (2 * pages + peers - 1) // peers)
    earlier = jnp.arange(pages)[:, None] > jnp.arange(pages)[None, :]
    ranks = jnp.sum(((owners[:, None] == owners[None, :]) & earlier).astype(jnp.int32), axis=1)
    slots = {0: (owners * capacity + ranks)[None]}
    for axis, bit, flag in (("grp", 1, 1), ("grp", 2, 2), ("tok", 1, 4)):
        slots[flag] = flipped(slots[0], axis, bit)
        slots[0] = jnp.concatenate([slots[0], slots[flag]], axis=0)
    slots = slots[0][jnp.arange(blocks) ^ member][:, None, :]

    first_row = place // PAIR * group_rows
    padded_ids = jnp.concatenate(
        [
            jnp.full((SPAN,), -1, jnp.int32),
            segment_ids,
            jnp.full((SPAN,), 1 << 30, jnp.int32),
        ]
    )
    window_ids = lax.dynamic_slice_in_dim(padded_ids, first_row, group_rows + 2 * SPAN, 0)
    starts, ends = document_bounds(window_ids, rows, blocks)
    positions = SPAN + jnp.arange(group_rows, dtype=jnp.int32) - starts
    cosine, sine = rope_tables(positions)
    ranges = jnp.stack(
        [starts[::TILE] // TILE, (ends[TILE - 1 :: TILE] + TILE - 1) // TILE], axis=1
    ).reshape(-1)

    order = [
        (number * members + column) % PARTS for number in range(PARTS)
    ]
    meta = jnp.stack([member, place] + order).astype(jnp.int32)
    queries, chunk_a, chunk_b, chunk_c, send = project(
        meta, layout, operands, weights, cosine, sine, slots, rows, peers, capacity
    )

    before = shifted(chunk_c, "tok", PAIR)
    after = shifted(chunk_a, "tok", -PAIR)
    received = lax.all_to_all(
        send.reshape((peers * members,) + send.shape[2:]),
        ("tok", "grp"),
        split_axis=0,
        concat_axis=0,
        tiled=True,
    )

    last_columns = lax.all_gather(output_weight, "tok", axis=0, tiled=True)
    queries, last_columns = lax.optimization_barrier((queries, last_columns))
    last_weight = lax.all_gather(last_columns, "grp", axis=0, tiled=True)

    bounds = (starts[None, :], ends[None, :])
    total, peaks = attend_local(ranges, queries, *bounds, (chunk_a, chunk_b, chunk_c))
    own_member = member[None].astype(jnp.int32)
    mixed = attend_finish(
        jnp.concatenate([own_member, ranges]),
        queries,
        *bounds,
        before,
        after,
        total,
        peaks,
        rows,
    )
    flat = peers * members
    parts = [mixed[0]] + [
        lax.ppermute(
            mixed[distance],
            ("tok", "grp"),
            [(source, source ^ distance) for source in range(flat)],
        )
        for distance in range(1, blocks)
    ]
    attended = output_projection(own_member, parts, last_weight)

    cache_pages = unpack(
        received.reshape((peers // PAIR, PAIR, members) + send.shape[2:])
    ).reshape(peers * capacity, 2 * PAGE * model_width)
    return attended, cache_pages


def solution(mesh):
    placed = (
        P(("tok", "grp"), None),
        P(),
        P("tok", "grp"),
        P("tok", "grp"),
        P(),
        P(("tok", "grp"), None),
    )
    return jax.shard_map(
        per_device,
        mesh=mesh,
        in_specs=placed,
        out_specs=(P(("tok", "grp"), None), P(("tok", "grp"), None)),
        check_vma=False,
    )
```

time: 468 us -> 273 us (0.58)
  the two profiles are of different devices: /device:TPU:3 before, /device:TPU:11 now
where the time goes in v2:
time: 273 us; the launch traced here: 272 us
  blocking collectives  88 us (32%)
  Pallas kernels  84.7 us (31%)
  starting transfers between devices  46.8 us (17%)
  waiting for transfers between devices  21.7 us (8%)
  between operations  14.6 us (5%)
  other arithmetic  8.56 us (3%)
  local copies, waits for them, and re-layouts  7.61 us (3%)
    all_gather x1, blocking collectives, per_device(): last_columns = lax.all_gather(output_weight, 'tok', axis=0, tiled=True)  88 us
    pallas_call x1, Pallas kernels, attend_local(): pl.pallas_call(attend_kernel, grid_spec=pltpu.PrefetchScalarGridSpec(num_...  42.5 us
    ppermute x16, starting transfers between devices, flipped(): lax.ppermute(value, axis, [(source, source ^ bit) for source in range(cou...  19.4 us
    pallas_call x1, Pallas kernels, attend_finish(): pl.pallas_call(finish_kernel, grid_spec=pltpu.PrefetchScalarGridSpec(num_...  14.4 us
    pallas_call x1, Pallas kernels, project(): pl.pallas_call(functools.partial(project_kernel, layout, len(weights), pe...  13.5 us
    ppermute x16, waiting for transfers between devices, flipped(): lax.ppermute(value, axis, [(source, source ^ bit) for source in range(cou...  13.3 us
    ppermute x7, starting transfers between devices, per_device(): lax.ppermute(mixed[distance], ('tok', 'grp'), [(source, source ^ distance...  10.9 us
    ppermute x7, waiting for transfers between devices, per_device(): lax.ppermute(mixed[distance], ('tok', 'grp'), [(source, source ^ distance...  7.41 us
  transfers between devices with their start and end apart: 30, of which 7 were waited for; matrix products, arithmetic and copies ran while one was open for 5% of the time, Pallas kernels for 23%

profile of v2, /device:TPU:11, one launch (start us, length us, event | category | flops | bytes accessed | tf_op | source)
XLA Modules:
  0.0 272.0 jit_solution(4722176248029146728)
XLA Ops:
  7.2 3.2 %layer_norm.1.refs_0_ = bf16[384,1024]{1,0:T(8,128)(2,1)} custom-call(bf16[384,1024]{1,0:T(8,128)(2,1)} %tokens.1, f32[1,1024]{1,0:T(1,128)} %bitcast.50), custom_call_target="tpu_custom_call" | custom-call | tf_op jit(solution)/shard_map/layer_norm/pallas_call | solution.py:49
  10.7 1.2 collective-permute-start.1
  15.2 1.5 collective-permute-start.16
  17.2 3.9 %convert_reduce_fusion.1 = (s32[8,384]{1,0:T(8,128)S(1)}, s32[8,384]{1,0:T(8,128)S(1)}) fusion(s32[8,384]{1,0:T(8,128)S(1)} %lt.56, s32[8,1408]{1,0:T(8,128)S(1)} %stack.87, s32[8,1408]{1,0:T(8,128)S(1)} %stack.97), kind=kLoop, calls=%fused_computation.2 | loop fusion | flops 25946112 | bytes 126976 | tf_op jit(solution)/shard_map/reduce_sum | solution.py:500
  21.3 9.8 %collective-permute-done.9 = bf16[128,3,128]{2,0,1:T(8,128)(2,1)S(1)} collective-permute-done((bf16[128,3,128]{2,0,1:T(8,128)(2,1)S(1)}, bf16[128,3,128]{2,0,1:T(8,128)(2,1)S(1)}, u32[]{:S(2)}, u32[]{:S(2)}) %collective-permute-start.9) | collective-permute-done | bytes 98336 | tf_op jit(solution)/shard_map/ppermute | solution.py:30
  31.1 3.1 %collective-permute-start.10 = (bf16[256,128]{1,0:T(8,128)(2,1)S(1)}, bf16[256,128]{1,0:T(8,128)(2,1)S(1)}, u32[]{:S(2)}, u32[]{:S(2)}) collective-permute-start(bf16[256,128]{1,0:T(8,128)(2,1)S(1)} %get-tuple-element.39), channel_id=1, source_target_pairs={{0,0},{1,3},{2,2},{3,1},{4,4},{5,7},{6,6},{7,5},{8,8},{9,11},{10,1... | collective-permute-start | bytes 196616 | tf_op jit(solution)/shard_map/ppermute | solution.py:525
  36.9 2.4 collective-permute-start.14
  39.3 1.3 collective-permute-start.2
  40.6 1.3 collective-permute-start.3
  42.1 1.8 collective-permute-done.14.refs_12_
  44.8 1.3 collective-permute-start.18
  46.1 1.7 collective-permute-done.18
  47.7 6.7 %collective-permute-start.4 = (bf16[384,1024]{1,0:T(8,128)(2,1)S(1)}, bf16[384,1024]{1,0:T(8,128)(2,1)}, u32[]{:S(2)}, u32[]{:S(2)}) collective-permute-start(bf16[384,1024]{1,0:T(8,128)(2,1)S(1)} %copy-done.1), channel_id=1, source_target_pairs={{0,1},{1,0},{2,3},{3,2},{4,5},{5,4},{6,7},{7,6},{8,9},{9,8},{10,11... | collective-permute-start | bytes 2359304 | tf_op jit(solution)/shard_map/ppermute | solution.py:30
  54.5 1.1 collective-permute-start.6
  56.3 2.3 multiply_sine_fusion
  59.2 1.1 gather_fusion
  60.4 13.5 %project.1 = (bf16[3072,128]{1,0:T(8,128)(2,1)}, bf16[1024,256]{1,0:T(8,128)(2,1)}, bf16[1024,256]{1,0:T(8,128)(2,1)}, bf16[1024,256]{1,0:T(8,128)(2,1)}, bf16[8,4,2,24,1024]{4,3,2,1,0:T(8,128)(2,1)}) custom-call(s32[5]{0:T(128)} %stack.104.meta, bf16[384,1024]{1,0:T(8,128)(2,1)} %layer_norm.1.refs_0_, bf16[384,1024]{1,0:T(8,128)(2,1)} %copy-done.2, ...), custom_call_target="tpu_custom_call" | custom-call | flops 2415919104 | bytes 12582912 | tf_op jit(solution)/shard_map/project/pallas_call | solution.py:170
  73.9 6.7 %all-to-all-start = ((bf16[32,2,24,1024]{3,2,1,0:T(8,128)(2,1)}), bf16[32,2,24,1024]{3,2,1,0:T(8,128)(2,1)S(1)}, u32[]{:S(2)}, u32[]{:S(2)}) async-start(bf16[32,2,24,1024]{3,2,1,0:T(8,128)(2,1)} %bitcast.40), calls=%async_computation | async-start | bytes 6291456 | tf_op jit(solution)/shard_map/all_to_all | solution.py:591
  80.7 88.0 %all_gather.6 = bf16[1024,256]{1,0:T(8,128)(2,1)} all-gather(bf16[128,256]{1,0:T(8,128)(2,1)S(1)} %copy-done.8), channel_id=1, replica_groups=mesh['tok'=8,'grp'=4] {'tok'}, dimensions={0}, use_global_device_ids=true | all-gather | bytes 589824 | tf_op jit(solution)/shard_map/all_gather | solution.py:599
  171.0 2.6 collective-permute-start.19
  173.6 2.7 collective-permute-start.20
  176.3 42.5 %attend_local.1 = (f32[12,160,256]{2,1,0:T(8,128)}, f32[12,8,256]{2,1,0:T(8,128)}) custom-call(s32[24]{0:T(128)} %copy-done.11, bf16[3072,128]{1,0:T(8,128)(2,1)} %get-tuple-element.20.queries, s32[1,3072]{1,0:T(1,128)} %bitcast.46, s32[1,3072]{1,0:T(1,128)} %bitcast.48, bf16[1024,256]{1,0:T(8,128)(2,1)} %get-tuple-element.22.chunk_a, ...), custom_call_target="tpu_custom_call" | custom-call | flops 6442450944 | bytes 5242880 | tf_op jit(solution)/shard_map/attend_local/pallas_call | solution.py:347
  219.5 14.4 %attend_finish.1 = (bf16[384,128]{1,0:T(8,128)(2,1)}, bf16[384,128]{1,0:T(8,128)(2,1)}, bf16[384,128]{1,0:T(8,128)(2,1)}, bf16[384,128]{1,0:T(8,128)(2,1)}, bf16...) custom-call(s32[25]{0:T(128)} %pad_add_fusion.4.meta, ...), custom_call_target="tpu_custom_call" | custom-call | flops 1610612736 | bytes 5242880 | tf_op jit(solution)/shard_map/attend_finish/pallas_call | solution.py:381
  234.0 5.5 %collective-permute-start.21 = (bf16[384,128]{1,0:T(8,128)(2,1)}, bf16[384,128]{1,0:T(8,128)(2,1)S(1)}, u32[]{:S(2)}, u32[]{:S(2)}) collective-permute-start(bf16[384,128]{1,0:T(8,128)(2,1)} %get-tuple-element.27), channel_id=1, source_target_pairs={{0,1},{1,0},{2,3},{3,2},{4,5},{5,4},{6,7},{7,6},{8,9},{9,8},{10,11... | collective-permute-start | bytes 294920 | tf_op jit(solution)/shard_map/ppermute | solution.py:618
  239.4 1.7 collective-permute-start.23
  241.7 1.2 collective-permute-start.25
  244.0 1.6 collective-permute-start.27
  245.6 1.5 collective-permute-done.23.refs_3_
  247.1 5.2 %collective-permute-done.25.refs_5_ = bf16[384,128]{1,0:T(8,128)(2,1)} collective-permute-done((bf16[384,128]{1,0:T(8,128)(2,1)}, bf16[384,128]{1,0:T(8,128)(2,1)}, u32[]{:S(2)}, u32[]{:S(2)}) %collective-permute-start.25) | collective-permute-done | bytes 98336 | tf_op jit(solution)/shard_map/ppermute | solution.py:618
  252.4 4.7 %output_projection.1 = bf16[384,1024]{1,0:T(8,128)(2,1)} custom-call(s32[1]{0:T(128)} %bitcast.meta, bf16[384,128]{1,0:T(8,128)(2,1)} %get-tuple-element.26.refs_0_, bf16[384,128]{1,0:T(8,128)(2,1)} %copy-done.4, bf16[384,128]{1,0:T(8,128)(2,1)} %copy-done.5, bf16[384,128]{1,0:T(8,128)(2,1)} %copy-done.6, bf16[384,128]{1,0:T(8,128)(2,1)} %copy-done.7, ...), custom_call_target="tpu_custom_call" | custom-call | flops 805306368 | bytes 4194304 | tf_op jit(solution)/shard_map/output_projection/pallas_call | solution.py:431
  257.1 1.6 copy-done
  258.7 6.4 %unpack.1 = bf16[8,24,8192]{2,1,0:T(8,128)(2,1)} custom-call(bf16[4,2,4,2,24,1024]{5,4,3,2,1,0:T(8,128)(2,1)} %bitcast.39), custom_call_target="tpu_custom_call" | custom-call | bytes 6291456 | tf_op jit(solution)/shard_map/unpack/pallas_call | solution.py:465
  (128 shorter events, 13.8 us)
Async XLA Ops:
  10.4 37.3 %copy-start.1 = (bf16[384,1024]{1,0:T(8,128)(2,1)S(1)}, bf16[384,1024]{1,0:T(8,128)(2,1)}, u32[]{:S(2)}) copy-start(bf16[384,1024]{1,0:T(8,128)(2,1)} %layer_norm.1.refs_0_) | copy-start | bytes 2359300
  10.4 28.8 %collective-permute-start = (bf16[384,1024]{1,0:T(8,128)(2,1)}, bf16[384,1024]{1,0:T(8,128)(2,1)S(1)}, u32[]{:S(2)}, u32[]{:S(2)}) collective-permute-start(bf16[384,1024]{1,0:T(8,128)(2,1)} %layer_norm.1.refs_0_), channel_id=1, source_target_pairs={{0,2},{1,3},{2,0},{3,1},{4,6},{5,7},{6,4},{7,5},{8,10},{9,11},{10,... | collective-permute-start | bytes 2359304 | tf_op jit(solution)/shard_map/ppermute | solution.py:30
  10.7 29.9 %collective-permute-start.1 = (bf16[384,1024]{1,0:T(8,128)(2,1)}, bf16[384,1024]{1,0:T(8,128)(2,1)S(1)}, u32[]{:S(2)}, u32[]{:S(2)}) collective-permute-start(bf16[384,1024]{1,0:T(8,128)(2,1)} %layer_norm.1.refs_0_), channel_id=1, source_target_pairs={{0,4},{4,0},{8,12},{12,8},{16,20},{20,16},{24,28},{28,24},{1,5},{5... | collective-permute-start | bytes 2359304 | tf_op jit(solution)/shard_map/ppermute | solution.py:30
  13.3 17.7 %collective-permute-start.9 = (bf16[128,3,128]{2,0,1:T(8,128)(2,1)S(1)}, bf16[128,3,128]{2,0,1:T(8,128)(2,1)S(1)}, u32[]{:S(2)}, u32[]{:S(2)}) collective-permute-start(bf16[128,3,128]{2,0,1:T(8,128)(2,1)S(1)} %bitcast.45), channel_id=1, source_target_pairs={{0,4},{4,0},{8,12},{12,8},{16,20},{20,16},{24,28},{28,24},{1,5},{5... | collective-permute-start | bytes 294920 | tf_op jit(solution)/shard_map/ppermute | solution.py:30
  15.2 19.0 %collective-permute-start.16 = (s32[1,96]{1,0:T(1,128)S(1)}, s32[1,96]{1,0:T(1,128)S(1)}, u32[]{:S(2)}, u32[]{:S(2)}) collective-permute-start(s32[1,96]{1,0:T(1,128)S(1)} %bitcast_add_fusion), channel_id=1, source_target_pairs={{0,1},{1,0},{2,3},{3,2},{4,5},{5,4},{6,7},{7,6},{8,9},{9,8},{10,11... | collective-permute-start | bytes 1160 | tf_op jit(solution)/shard_map/ppermute | solution.py:30
  31.1 5.0 %collective-permute-start.10 = (bf16[256,128]{1,0:T(8,128)(2,1)S(1)}, bf16[256,128]{1,0:T(8,128)(2,1)S(1)}, u32[]{:S(2)}, u32[]{:S(2)}) collective-permute-start(bf16[256,128]{1,0:T(8,128)(2,1)S(1)} %get-tuple-element.39), channel_id=1, source_target_pairs={{0,0},{1,3},{2,2},{3,1},{4,4},{5,7},{6,6},{7,5},{8,8},{9,11},{10,1... | collective-permute-start | bytes 196616 | tf_op jit(solution)/shard_map/ppermute | solution.py:525
  34.2 10.5 %collective-permute-start.17 = (s32[2,96]{1,0:T(2,128)S(1)}, s32[2,96]{1,0:T(2,128)S(1)}, u32[]{:S(2)}, u32[]{:S(2)}) collective-permute-start(s32[2,96]{1,0:T(2,128)S(1)} %pad_add_fusion.3), channel_id=1, source_target_pairs={{0,2},{1,3},{2,0},{3,1},{4,6},{5,7},{6,4},{7,5},{8,10},{9,11},{10,... | collective-permute-start | bytes 2312 | tf_op jit(solution)/shard_map/ppermute | solution.py:30
  34.6 2.2 collective-permute-start.11
  36.1 0.7 collective-permute-start.12
  36.9 23.5 %copy-start.10 = (bf16[256,384]{1,0:T(8,128)(2,1)}, bf16[256,384]{1,0:T(8,128)(2,1)S(1)}, u32[]{:S(2)}) copy-start(bf16[256,384]{1,0:T(8,128)(2,1)S(1)} %constant_dynamic-update-slice_fusion.refs_10_) | copy-start | bytes 589828
  36.9 7.0 %collective-permute-start.14 = (bf16[256,384]{1,0:T(8,128)(2,1)S(1)}, bf16[256,384]{1,0:T(8,128)(2,1)S(1)}, u32[]{:S(2)}, u32[]{:S(2)}) collective-permute-start(bf16[256,384]{1,0:T(8,128)(2,1)S(1)} %constant_dynamic-update-slice_fusion.refs_10_), channel_id=1, source_target_pairs={{0,16},{4,20},{8,24},{12,28},{16,0},{20,4},{24,8},{28,12},{1,17},{... | collective-permute-start | bytes 589832 | tf_op jit(solution)/shard_map/ppermute | solution.py:30
  39.3 16.3 %collective-permute-start.2 = (bf16[192,1024]{1,0:T(8,128)(2,1)S(1)}, bf16[192,1024]{1,0:T(8,128)(2,1)}, u32[]{:S(2)}, u32[]{:S(2)}) collective-permute-start(bf16[192,1024]{1,0:T(8,128)(2,1)S(1)} %slice.115), channel_id=1, source_target_pairs={{0,4},{4,0},{8,12},{12,8},{16,20},{20,16},{24,28},{28,24},{1,5},{5... | collective-permute-start | bytes 1179656 | tf_op jit(solution)/shard_map/ppermute | solution.py:30
  40.6 15.1 %collective-permute-start.3 = (bf16[192,1024]{1,0:T(8,128)(2,1)S(1)}, bf16[192,1024]{1,0:T(8,128)(2,1)}, u32[]{:S(2)}, u32[]{:S(2)}) collective-permute-start(bf16[192,1024]{1,0:T(8,128)(2,1)S(1)} %slice.116), channel_id=1, source_target_pairs={{0,2},{1,3},{2,0},{3,1},{4,6},{5,7},{6,4},{7,5},{8,10},{9,11},{10,... | collective-permute-start | bytes 1179656 | tf_op jit(solution)/shard_map/ppermute | solution.py:30
  41.9 12.5 %collective-permute-start.13 = (bf16[256,384]{1,0:T(8,128)(2,1)S(1)}, bf16[256,384]{1,0:T(8,128)(2,1)S(1)}, u32[]{:S(2)}, u32[]{:S(2)}) collective-permute-start(bf16[256,384]{1,0:T(8,128)(2,1)S(1)} %constant_dynamic-update-slice_fusion.refs_10_), channel_id=1, source_target_pairs={{0,8},{4,12},{8,0},{12,4},{16,24},{20,28},{24,16},{28,20},{1,9},{5... | collective-permute-start | bytes 589832 | tf_op jit(solution)/shard_map/ppermute | solution.py:30
  43.9 10.6 %collective-permute-start.15 = (bf16[256,384]{1,0:T(8,128)(2,1)S(1)}, bf16[256,384]{1,0:T(8,128)(2,1)S(1)}, u32[]{:S(2)}, u32[]{:S(2)}) collective-permute-start(bf16[256,384]{1,0:T(8,128)(2,1)S(1)} %collective-permute-done.14.refs_12_), channel_id=1, source_target_pairs={{0,8},{4,12},{8,0},{12,4},{16,24},{20,28},{24,16},{28,20},{1,9},{5... | collective-permute-start | bytes 589832 | tf_op jit(solution)/shard_map/ppermute | solution.py:30
  44.8 2.9 %collective-permute-start.18 = (s32[4,96]{1,0:T(4,128)S(1)}, s32[4,96]{1,0:T(4,128)S(1)}, u32[]{:S(2)}, u32[]{:S(2)}) collective-permute-start(s32[4,96]{1,0:T(4,128)S(1)} %pad_add_fusion.1), channel_id=1, source_target_pairs={{0,4},{4,0},{8,12},{12,8},{16,20},{20,16},{24,28},{28,24},{1,5},{5... | collective-permute-start | bytes 4616 | tf_op jit(solution)/shard_map/ppermute | solution.py:30
  47.7 12.6 %collective-permute-start.4 = (bf16[384,1024]{1,0:T(8,128)(2,1)S(1)}, bf16[384,1024]{1,0:T(8,128)(2,1)}, u32[]{:S(2)}, u32[]{:S(2)}) collective-permute-start(bf16[384,1024]{1,0:T(8,128)(2,1)S(1)} %copy-done.1), channel_id=1, source_target_pairs={{0,1},{1,0},{2,3},{3,2},{4,5},{5,4},{6,7},{7,6},{8,9},{9,8},{10,11... | collective-permute-start | bytes 2359304 | tf_op jit(solution)/shard_map/ppermute | solution.py:30
  54.4 5.9 %collective-permute-start.5 = (bf16[384,1024]{1,0:T(8,128)(2,1)S(1)}, bf16[384,1024]{1,0:T(8,128)(2,1)}, u32[]{:S(2)}, u32[]{:S(2)}) collective-permute-start(bf16[384,1024]{1,0:T(8,128)(2,1)S(1)} %collective-permute-done.refs_1_), channel_id=1, source_target_pairs={{0,1},{1,0},{2,3},{3,2},{4,5},{5,4},{6,7},{7,6},{8,9},{9,8},{10,11... | collective-permute-start | bytes 2359304 | tf_op jit(solution)/shard_map/ppermute | solution.py:30
  54.5 5.9 %collective-permute-start.6 = (bf16[384,1024]{1,0:T(8,128)(2,1)S(1)}, bf16[384,1024]{1,0:T(8,128)(2,1)}, u32[]{:S(2)}, u32[]{:S(2)}) collective-permute-start(bf16[384,1024]{1,0:T(8,128)(2,1)S(1)} %collective-permute-done.1.refs_2_), channel_id=1, source_target_pairs={{0,1},{1,0},{2,3},{3,2},{4,5},{5,4},{6,7},{7,6},{8,9},{9,8},{10,11... | collective-permute-start | bytes 2359304 | tf_op jit(solution)/shard_map/ppermute | solution.py:30
  55.6 4.8 %collective-permute-start.7 = (bf16[192,1024]{1,0:T(8,128)(2,1)}, bf16[192,1024]{1,0:T(8,128)(2,1)}, u32[]{:S(2)}, u32[]{:S(2)}) collective-permute-start(bf16[192,1024]{1,0:T(8,128)(2,1)} %collective-permute-done.2.refs_3_), channel_id=1, source_target_pairs={{0,1},{1,0},{2,3},{3,2},{4,5},{5,4},{6,7},{7,6},{8,9},{9,8},{10,11... | collective-permute-start | bytes 1179656 | tf_op jit(solution)/shard_map/ppermute | solution.py:30
  55.7 4.7 %collective-permute-start.8 = (bf16[192,1024]{1,0:T(8,128)(2,1)}, bf16[192,1024]{1,0:T(8,128)(2,1)}, u32[]{:S(2)}, u32[]{:S(2)}) collective-permute-start(bf16[192,1024]{1,0:T(8,128)(2,1)} %collective-permute-done.3.refs_4_), channel_id=1, source_target_pairs={{0,1},{1,0},{2,3},{3,2},{4,5},{5,4},{6,7},{7,6},{8,9},{9,8},{10,11... | collective-permute-start | bytes 1179656 | tf_op jit(solution)/shard_map/ppermute | solution.py:30
  73.9 183.1 %all-to-all-start = ((bf16[32,2,24,1024]{3,2,1,0:T(8,128)(2,1)}), bf16[32,2,24,1024]{3,2,1,0:T(8,128)(2,1)S(1)}, u32[]{:S(2)}, u32[]{:S(2)}) async-start(bf16[32,2,24,1024]{3,2,1,0:T(8,128)(2,1)} %bitcast.40), calls=%async_computation | async-start | bytes 6291456 | tf_op jit(solution)/shard_map/all_to_all | solution.py:591
  80.6 171.7 %all-gather.2.cloned.1.call-start = ((), (), s32[]{:S(2)}) async-start(), calls=%async_computation.1 | async-start | bytes 2621440 | tf_op jit(solution)/shard_map/all_gather | solution.py:601
  171.0 47.8 %collective-permute-start.19 = (bf16[1024,256]{1,0:T(8,128)(2,1)}, bf16[1024,256]{1,0:T(8,128)(2,1)S(1)}, u32[]{:S(2)}, u32[]{:S(2)}) collective-permute-start(bf16[1024,256]{1,0:T(8,128)(2,1)} %get-tuple-element.21.chunk_c), channel_id=1, source_target_pairs={{0,8},{4,12},{8,16},{12,20},{16,24},{20,28},{1,9},{5,13},{9,17},{1... | collective-permute-start | bytes 1572872 | tf_op jit(solution)/shard_map/ppermute | solution.py:36
  173.6 45.2 %collective-permute-start.20 = (bf16[1024,256]{1,0:T(8,128)(2,1)}, bf16[1024,256]{1,0:T(8,128)(2,1)}, u32[]{:S(2)}, u32[]{:S(2)}) collective-permute-start(bf16[1024,256]{1,0:T(8,128)(2,1)} %get-tuple-element.22.chunk_a), channel_id=1, source_target_pairs={{8,0},{12,4},{16,8},{20,12},{24,16},{28,20},{9,1},{13,5},{17,9},{2... | collective-permute-start | bytes 1572872 | tf_op jit(solution)/shard_map/ppermute | solution.py:36
  234.0 9.0 %collective-permute-start.21 = (bf16[384,128]{1,0:T(8,128)(2,1)}, bf16[384,128]{1,0:T(8,128)(2,1)S(1)}, u32[]{:S(2)}, u32[]{:S(2)}) collective-permute-start(bf16[384,128]{1,0:T(8,128)(2,1)} %get-tuple-element.27), channel_id=1, source_target_pairs={{0,1},{1,0},{2,3},{3,2},{4,5},{5,4},{6,7},{7,6},{8,9},{9,8},{10,11... | collective-permute-start | bytes 294920 | tf_op jit(solution)/shard_map/ppermute | solution.py:618
  239.4 4.6 %collective-permute-start.22 = (bf16[384,128]{1,0:T(8,128)(2,1)}, bf16[384,128]{1,0:T(8,128)(2,1)S(1)}, u32[]{:S(2)}, u32[]{:S(2)}) collective-permute-start(bf16[384,128]{1,0:T(8,128)(2,1)} %get-tuple-element.28), channel_id=1, source_target_pairs={{0,2},{1,3},{2,0},{3,1},{4,6},{5,7},{6,4},{7,5},{8,10},{9,11},{10,... | collective-permute-start | bytes 294920 | tf_op jit(solution)/shard_map/ppermute | solution.py:618
  239.4 7.6 %collective-permute-start.23 = (bf16[384,128]{1,0:T(8,128)(2,1)}, bf16[384,128]{1,0:T(8,128)(2,1)S(1)}, u32[]{:S(2)}, u32[]{:S(2)}) collective-permute-start(bf16[384,128]{1,0:T(8,128)(2,1)} %get-tuple-element.29), channel_id=1, source_target_pairs={{0,3},{1,2},{2,1},{3,0},{4,7},{5,6},{6,5},{7,4},{8,11},{9,10},{10,... | collective-permute-start | bytes 294920 | tf_op jit(solution)/shard_map/ppermute | solution.py:618
  241.1 5.9 %collective-permute-start.24 = (bf16[384,128]{1,0:T(8,128)(2,1)}, bf16[384,128]{1,0:T(8,128)(2,1)S(1)}, u32[]{:S(2)}, u32[]{:S(2)}) collective-permute-start(bf16[384,128]{1,0:T(8,128)(2,1)} %get-tuple-element.30), channel_id=1, source_target_pairs={{0,4},{1,5},{2,6},{3,7},{4,0},{5,1},{6,2},{7,3},{8,12},{9,13},{10,... | collective-permute-start | bytes 294920 | tf_op jit(solution)/shard_map/ppermute | solution.py:618
  241.7 10.6 %collective-permute-start.25 = (bf16[384,128]{1,0:T(8,128)(2,1)}, bf16[384,128]{1,0:T(8,128)(2,1)}, u32[]{:S(2)}, u32[]{:S(2)}) collective-permute-start(bf16[384,128]{1,0:T(8,128)(2,1)} %get-tuple-element.31), channel_id=1, source_target_pairs={{0,5},{1,4},{2,7},{3,6},{4,1},{5,0},{6,3},{7,2},{8,13},{9,12},{10,... | collective-permute-start | bytes 294920 | tf_op jit(solution)/shard_map/ppermute | solution.py:618
  242.9 9.4 %collective-permute-start.26 = (bf16[384,128]{1,0:T(8,128)(2,1)}, bf16[384,128]{1,0:T(8,128)(2,1)}, u32[]{:S(2)}, u32[]{:S(2)}) collective-permute-start(bf16[384,128]{1,0:T(8,128)(2,1)} %get-tuple-element.32), channel_id=1, source_target_pairs={{0,6},{1,7},{2,4},{3,5},{4,2},{5,3},{6,0},{7,1},{8,14},{9,15},{10,... | collective-permute-start | bytes 294920 | tf_op jit(solution)/shard_map/ppermute | solution.py:618
  244.0 8.3 %collective-permute-start.27 = (bf16[384,128]{1,0:T(8,128)(2,1)}, bf16[384,128]{1,0:T(8,128)(2,1)}, u32[]{:S(2)}, u32[]{:S(2)}) collective-permute-start(bf16[384,128]{1,0:T(8,128)(2,1)} %get-tuple-element.33), channel_id=1, source_target_pairs={{0,7},{1,6},{2,5},{3,4},{4,3},{5,2},{6,1},{7,0},{8,15},{9,14},{10,... | collective-permute-start | bytes 294920 | tf_op jit(solution)/shard_map/ppermute | solution.py:618
  (14 other events, 118.9 us)
Sparse Core Ops, SparseCore 0:
  168.9 26.8 all-gather.1
